TPU v7x, 32 devices: a whole 2x2x4 slice. The times are simulated.
32 devices in a mesh: grp: 2 (over y), slab: 4 (over z), mem: 2 (over x), sub: 2 (over core).
Axes of the slice: x: 2, y: 2, z: 4, core: 2. Of those that a mesh axis runs over, the one named last changes fastest.
Arguments:
- state: bfloat16 [256, 32768], P('mem', ('grp', 'slab', 'sub')), parts along dimension 1, may hold values from -6 to 6
- centers: int32 [512], P('grp'), parts along dimension 0, may hold values from 0 to 16383, as said below
- half_width: int32 [512], P('grp'), parts along dimension 0, may hold values from 4 to 71
- radius: int32 [512], P('grp'), parts along dimension 0, may hold values from 2048 to 8192
- order: int32 [512], P('grp'), parts along dimension 0, may hold values from 0 to 255, each once
- obs_var: float32 [512], P('grp'), parts along dimension 0, may hold values from 0.1 to 1
Outputs:
- analysis: bfloat16 [256, 32768], P('mem', ('grp', 'slab', 'sub')), parts along dimension 1
There are 2 independent parts, one for each index of `grp`. A program takes and returns all parts, laid end to end along the dimension named above; each array names one. Nothing has to cross between parts.
Inputs may be any that keep to these rules, and one draw needn't show every extreme that they name: order holds every observation number once. Observations 4 k to 4 k + 3 have centers within 6 rows of a common site row, which the first of them sits on; centers are clipped to the grid.
All inputs are finite; a program needn't handle non-finite values.
Results may differ from a plain program's by a relative error of at most 0.0049.
Values may be sent and summed in bfloat16 or wider, within the bound.
A program may use at most 64 MiB of HBM per device.

v0:
```python
import functools
import math

import jax
import jax.numpy as jnp
from jax import lax
from jax.experimental import pallas as pl
from jax.experimental.pallas import tpu as pltpu
from jax.sharding import PartitionSpec as P

M = 256
P_SIZE = 128
BATCHES = 2
BLOCK = 16
SPLIT = 4
SPLIT_2 = 4

FLOOR = math.exp(-2.0)
F32 = jnp.float32
BF16 = jnp.bfloat16
HIGH = lax.Precision.HIGHEST
LAST = (((1,), (1,)), ((), ()))
FIRST = (((0,), (0,)), ((), ()))


def each(start, stop, body):
    if stop - start <= 16:
        for i in range(start, stop):
            body(i)
    else:

        def step(i, carry):
            body(i)
            return carry

        lax.fori_loop(start, stop, step, 0)


def split3(x):
    high = x.astype(BF16)
    rest = x - high.astype(F32)
    mid = rest.astype(BF16)
    low = (rest - mid.astype(F32)).astype(BF16)
    return high, mid, low


def sweep(work, inv, solved, root, first=0, last=P_SIZE // BLOCK):
    b = BLOCK
    width = work.shape[1] // P_SIZE

    def step(k, carry):
        r0 = pl.multiple_of(k * b, b)
        parts = [work[pl.ds(r0, b), g * P_SIZE : (g + 1) * P_SIZE] for g in range(width)]
        roots = root[pl.ds(r0, b), :]
        rolled = pltpu.roll(parts[0], lax.rem(P_SIZE - r0, P_SIZE), 1)
        cols = [jnp.broadcast_to(rolled[:, j : j + 1], (b, P_SIZE)) for j in range(b)]
        row_id = lax.broadcasted_iota(jnp.int32, (b, P_SIZE), 0)
        for j in range(b):
            pivot = cols[j][j : j + 1, :]
            scale = lax.rsqrt(pivot)
            scale_m = 1.0 / (pivot * scale + roots[j : j + 1, :])
            column = jnp.where(row_id > j, cols[j] * scale, 0.0)
            for i in range(j + 1, b):
                cols[i] = cols[i] - column * column[i : i + 1, :]
            for g in range(width):
                row = parts[g][j : j + 1, :] * (scale if g < 2 else scale_m)
                parts[g] = jnp.where(row_id == j, row, parts[g] - column * row)
        inv[pl.ds(r0, b), :] = parts[1]
        for g in range(2, width):
            solved[pl.ds(r0, b), (g - 2) * P_SIZE : (g - 1) * P_SIZE] = parts[g]
        pieces = [split3(x) for x in parts]
        h, m, l = pieces[0]
        left = jnp.concatenate([h, h, m, h, m, l], axis=0)
        h, m, l = (jnp.concatenate([x[n] for x in pieces], axis=1) for n in range(3))
        right = jnp.concatenate([h, m, h, l, m, h], axis=0)
        work[...] -= lax.dot_general(left, right, FIRST, preferred_element_type=F32)
        return carry

    lax.fori_loop(first, last, step, 0)


def kernel(
    shape,
    state_hbm, cen_hbm, half_hbm, rad_hbm, order_hbm, var_hbm,
    out,
    state, cen, half, rad, order, var,
    e_all, foot, tap, tap1, col_c, col_r, var_b, root_b, work, inv, solved, wts,
    part, rs, ag, cpart, crs, cag,
    in_s, e_ss, e_rs, t_ss, t_rs, rs_ss, rs_rs, crs_ss, crs_rs, ag_ss, ag_rs, cag_ss, cag_rs,
):
    n_slab, n_mem, n_sub = shape
    n = n_slab * n_sub
    total = n * n_mem
    own, rows = state.shape
    part_rows = rows // n_mem

    mi = lax.axis_index("mem")
    me = lax.axis_index("slab") * n_sub + lax.axis_index("sub")

    def peer(red, mem):
        return {"slab": lax.div(red, n_sub), "sub": lax.rem(red, n_sub), "mem": mem}

    def peer_of(off):
        red = lax.rem(me + lax.rem(off, n), n)
        mem = lax.rem(mi + lax.div(off, n), n_mem)
        return red, mem

    inputs = [
        pltpu.make_async_copy(a, b, in_s.at[i])
        for i, (a, b) in enumerate(
            zip(
                (state_hbm, cen_hbm, half_hbm, rad_hbm, order_hbm, var_hbm),
                (state, cen, half, rad, order, var),
            )
        )
    ]
    for copy in inputs[1:] + inputs[:1]:
        copy.start()

    barrier = pltpu.get_barrier_semaphore()

    def greet(off):
        red, mem = peer_of(off)
        pl.semaphore_signal(
            barrier, inc=1, device_id=peer(red, mem), device_id_type=pl.DeviceIdType.MESH
        )

    each(1, total, greet)
    for copy in inputs[1:]:
        copy.wait()

    n_obs = BATCHES * P_SIZE
    picked = jnp.broadcast_to(order[...].astype(F32), (P_SIZE, n_obs)).T.astype(jnp.int32)
    lane = lax.broadcasted_iota(jnp.int32, (n_obs, P_SIZE), 1)
    masks = [picked == lane + h * P_SIZE for h in range(BATCHES)]

    def pick(ref):
        value = ref[...].astype(F32)
        chosen = 0.0
        for h in range(BATCHES):
            chosen = chosen + jnp.where(masks[h], value[:, h * P_SIZE : (h + 1) * P_SIZE], 0.0)
        return jnp.sum(chosen, axis=1, keepdims=True)

    center = pick(cen) - (me * rows).astype(F32)
    width = pick(half)
    variance = pick(var)
    col_c[...] = jnp.broadcast_to(center, (n_obs, P_SIZE))
    col_r[...] = jnp.broadcast_to(1.0 / pick(rad), (n_obs, P_SIZE))
    var_b[...] = jnp.broadcast_to(variance, (n_obs, P_SIZE))
    root_b[...] = jnp.broadcast_to(jnp.sqrt(variance), (n_obs, P_SIZE))
    steep = -2.0 / (width * width)
    height = 1.0 / jnp.sqrt(width)

    def rows_of(mem):
        return pl.ds(pl.multiple_of(mem * part_rows, part_rows), part_rows)

    my_rows = rows_of(mi)

    def e_copy(off):
        to = lax.rem(mi + off, n_mem)
        return pltpu.make_async_remote_copy(
            src_ref=state_hbm.at[:, rows_of(to)],
            dst_ref=e_all.at[mi],
            send_sem=e_ss.at[off],
            recv_sem=e_rs.at[mi],
            device_id=peer(me, to),
            device_id_type=pl.DeviceIdType.MESH,
        )

    def foot_tile(t, carry):
        at = pl.multiple_of(t * 256, 256)
        row = lax.broadcasted_iota(jnp.int32, (n_obs, 256), 1) + at
        distance = row.astype(F32) - center
        shape_f = jnp.maximum(jnp.exp(distance * distance * steep) - FLOOR, 0.0) * height
        foot[:, pl.ds(at, 256)] = shape_f.astype(BF16)
        return carry

    lax.fori_loop(0, rows // 256, foot_tile, 0)
    inputs[0].wait()
    sums = lax.dot_general(foot[...], state[...], LAST, preferred_element_type=F32)
    for b in range(BATCHES):
        part[b] = sums[b * P_SIZE : (b + 1) * P_SIZE, :].reshape(part.shape[1:])

    class Sum:
        def __init__(self, size, index, device, source, target, result, everyone, sems):
            self.size, self.index, self.device = size, index, device
            self.source, self.target, self.result, self.everyone = source, target, result, everyone
            self.rs_ss, self.rs_rs, self.ag_ss, self.ag_rs = sems
            self.owners = source.shape[0]
            self.stride = size // self.owners
            self.mine = lax.div(index, self.stride)

        def remote(self, src, dst, send, recv, device):
            return pltpu.make_async_remote_copy(
                src_ref=src, dst_ref=dst, send_sem=send, recv_sem=recv,
                device_id=device, device_id_type=pl.DeviceIdType.MESH,
            )

        def if_owner(self, body, owner=True):
            if self.stride == 1:
                if owner:
                    body()
            else:
                pl.when((lax.rem(self.index, self.stride) == 0) == owner)(body)

        def out_copy(self, off):
            o = lax.rem(self.mine + off, self.owners)
            return self.remote(
                self.source.at[o], self.target.at[self.index],
                self.rs_ss.at[off], self.rs_rs.at[self.index], self.device(o * self.stride),
            )

        def start(self):
            each(1, self.owners, lambda off: self.out_copy(off).start())
            self.if_owner(lambda: self.out_copy(0).start(), False)

        def gather_copy(self, off):
            block = self.result(mi, self.mine)
            return self.remote(
                block, block, self.ag_ss.at[off],
                self.ag_rs.at[mi if self.everyone else 0, self.mine], peer(*peer_of(off)),
            )

        def finish(self):
            def body():
                for off in range(1, self.size) if self.size <= 16 else ():
                    self.arrived(lax.rem(self.index + off, self.size))
                block = self.result(mi, self.mine)
                value = self.source[self.mine]
                if self.size <= 16:
                    for off in range(1, self.size):
                        value = value + self.target[lax.rem(self.index + off, self.size)]
                    block[...] = value
                else:
                    block[...] = value

                    def add(off):
                        src = lax.rem(self.index + off, self.size)
                        self.arrived(src)
                        block[...] += self.target[src]

                    each(1, self.size, add)
                each(1, total, lambda off: self.gather_copy(off).start())

            self.if_owner(body)

        def arrived(self, src):
            self.remote(
                self.source.at[0], self.target.at[src], self.rs_ss.at[0], self.rs_rs.at[src],
                self.device(src),
            ).wait_recv()

        def gather(self):
            mems = n_mem if self.everyone else 1

            def one(q):
                o = lax.rem(self.mine + lax.rem(q, self.owners), self.owners)
                mem = lax.rem(mi + lax.div(q, self.owners), n_mem)
                block = self.result(mem, o)
                self.remote(
                    block, block, self.ag_ss.at[0],
                    self.ag_rs.at[mem if self.everyone else 0, o],
                    self.device(o * self.stride),
                ).wait_recv()

            each(1, mems * self.owners, one)
            self.if_owner(lambda: one(0), False)

        def sent(self):
            each(1, self.owners, lambda off: self.out_copy(off).wait_send())
            self.if_owner(lambda: self.out_copy(0).wait_send(), False)
            self.if_owner(
                lambda: each(1, total, lambda off: self.gather_copy(off).wait_send())
            )

    projections = [
        Sum(
            n, me, lambda i: peer(i, mi), part.at[b], rs.at[b],
            lambda mem, o, b=b: ag.at[b, mem, o], True,
            (rs_ss.at[b], rs_rs.at[b], ag_ss.at[b], ag_rs.at[b]),
        )
        for b in range(BATCHES)
    ]
    changes = Sum(
        total, mi * n + me, lambda i: peer(lax.rem(i, n), lax.div(i, n)), cpart, crs,
        lambda mem, o: cag.at[o], False, (crs_ss, crs_rs, cag_ss, cag_rs),
    )
    pl.semaphore_wait(barrier, total - 1)
    for x in projections:
        x.start()
    each(1, n_mem, lambda off: e_copy(off).start())
    e_all[mi] = state[:, my_rows]
    projections[0].finish()

    def slot(b, s):
        return ag[b, s].reshape(P_SIZE, own)

    def load_work(columns, b):
        cov = 0.0
        for s in range(n_mem):
            cov = cov + lax.dot_general(
                columns[s], columns[s], LAST, precision=HIGH, preferred_element_type=F32
            )
        r = lax.broadcasted_iota(jnp.int32, (P_SIZE, P_SIZE), 0)
        eye = r == lax.broadcasted_iota(jnp.int32, (P_SIZE, P_SIZE), 1)
        v = var_b[b * P_SIZE : (b + 1) * P_SIZE, :]
        work[:, :P_SIZE] = cov * (1.0 / (M - 1)) + jnp.where(eye, v, 0.0)
        work[:, P_SIZE : 2 * P_SIZE] = jnp.where(eye, 1.0, 0.0)
        for s in range(n_mem):
            lo = 2 * P_SIZE + s * own
            work[:, lo : lo + own] = columns[s]

    def taper(b):
        lo = b * P_SIZE
        row = lax.broadcasted_iota(jnp.int32, (P_SIZE, part_rows), 1) + mi * part_rows
        c = jnp.concatenate([col_c[lo : lo + P_SIZE, :]] * (part_rows // P_SIZE), axis=1)
        r = jnp.concatenate([col_r[lo : lo + P_SIZE, :]] * (part_rows // P_SIZE), axis=1)
        near = jnp.maximum(1.0 - jnp.abs(row.astype(F32) - c) * r, 0.0)
        return near * near * (1.0 / (M - 1))

    def t_copy(x, ref, off):
        return pltpu.make_async_remote_copy(
            src_ref=ref.at[mi],
            dst_ref=ref.at[mi],
            send_sem=t_ss.at[x, off],
            recv_sem=t_rs.at[x, mi],
            device_id=peer(me, lax.rem(mi + off, n_mem)),
            device_id_type=pl.DeviceIdType.MESH,
        )

    def t_wait(x, ref, off):
        src = lax.rem(mi + off, n_mem)
        pltpu.make_async_remote_copy(
            src_ref=ref.at[src],
            dst_ref=ref.at[src],
            send_sem=t_ss.at[x, 0],
            recv_sem=t_rs.at[x, src],
            device_id=peer(me, src),
            device_id_type=pl.DeviceIdType.MESH,
        ).wait_recv()

    projections[0].gather()
    first = [slot(0, s) for s in range(n_mem)]
    first_b = [x.astype(BF16) for x in first]

    def e_wait(off):
        src = lax.rem(mi + off, n_mem)
        pltpu.make_async_remote_copy(
            src_ref=e_all.at[src],
            dst_ref=e_all.at[src],
            send_sem=e_ss.at[0],
            recv_sem=e_rs.at[src],
            device_id=peer(me, src),
            device_id_type=pl.DeviceIdType.MESH,
        ).wait_recv()

    each(1, n_mem, e_wait)

    cross = 0.0
    for s in range(n_mem):
        cross = cross + jnp.dot(first_b[s], e_all[s], preferred_element_type=F32)
    before = (taper(0) * cross).astype(BF16)
    tap[mi] = before
    change = lax.dot_general(
        foot[P_SIZE : 2 * P_SIZE, my_rows], before, LAST, preferred_element_type=F32
    )
    cpart[...] = change.reshape(cpart.shape)
    changes.start()
    projections[1].finish()

    load_work(first, 0)
    sweep(work, inv, solved, root_b.at[pl.ds(0, P_SIZE)], 0, SPLIT)
    changes.finish()
    each(1, n_mem, lambda off: t_copy(0, tap, off).start())
    sweep(work, inv, solved, root_b.at[pl.ds(0, P_SIZE)], SPLIT)

    def weights():
        return lax.dot_general(
            solved[...], inv[...], FIRST, precision=HIGH, preferred_element_type=F32
        )

    wts[...] = weights().astype(BF16)

    projections[1].gather()
    changes.gather()
    c_full = cag[...].reshape(P_SIZE, P_SIZE)
    second = []
    for s in range(n_mem):
        moved = lax.dot_general(
            c_full,
            wts[s * own : (s + 1) * own, :].astype(F32),
            LAST,
            precision=HIGH,
            preferred_element_type=F32,
        )
        second.append(slot(1, s) - moved)
    second_b = [x.astype(BF16) for x in second]

    before = tap[mi]
    cross = 0.0
    for s in range(n_mem):
        moved = jnp.dot(wts[s * own : (s + 1) * own, :], before, preferred_element_type=F32)
        now = (e_all[s].astype(F32) - moved).astype(BF16)
        cross = cross + jnp.dot(second_b[s], now, preferred_element_type=F32)
    tap1[mi] = (taper(1) * cross).astype(BF16)
    each(1, n_mem, lambda off: t_copy(1, tap1, off).start())

    load_work(second, 1)
    own_w = wts[pl.ds(pl.multiple_of(mi * own, own), own), :]
    sweep(work, inv, solved, root_b.at[pl.ds(P_SIZE, P_SIZE)], 0, SPLIT_2)
    each(1, n_mem, lambda off: t_wait(0, tap, off))
    for mem in range(n_mem):
        at = slice(mem * part_rows, (mem + 1) * part_rows)
        moved = jnp.dot(own_w, tap[mem], preferred_element_type=F32)
        out[:, at] = (state[:, at].astype(F32) - moved).astype(BF16)
    sweep(work, inv, solved, root_b.at[pl.ds(P_SIZE, P_SIZE)], SPLIT_2)
    wts[...] = weights().astype(BF16)
    own_w = wts[pl.ds(pl.multiple_of(mi * own, own), own), :]

    for off in range(n_mem):
        if off:
            t_wait(1, tap1, off)
        mem = lax.rem(mi + off, n_mem)
        at = rows_of(mem)
        moved = jnp.dot(own_w, tap1[mem], preferred_element_type=F32)
        out[:, at] = (out[:, at].astype(F32) - moved).astype(BF16)

    each(1, n_mem, lambda off: e_copy(off).wait_send())
    for x, ref in enumerate((tap, tap1)):
        each(1, n_mem, lambda off: t_copy(x, ref, off).wait_send())
    for x in projections + [changes]:
        x.sent()


def on_device(shape, state, centers, half_width, radius, order, obs_var):
    n_slab, n_mem, n_sub = shape
    own, rows = state.shape
    n = n_slab * n_sub
    total = n * n_mem
    owners = min(n, 4)
    chunk = P_SIZE // owners
    c_owners = min(total, 8)
    c_chunk = P_SIZE // c_owners
    n_obs = BATCHES * P_SIZE
    part_rows = rows // n_mem
    hbm = pl.BlockSpec(memory_space=pltpu.HBM)
    vmem = pl.BlockSpec(memory_space=pltpu.VMEM)
    return pl.pallas_call(
        functools.partial(kernel, shape),
        out_shape=jax.ShapeDtypeStruct((own, rows), BF16),
        in_specs=[hbm] * 6,
        out_specs=vmem,
        scratch_shapes=[
            pltpu.VMEM((own, rows), BF16),
            pltpu.VMEM((1, n_obs), jnp.int32),
            pltpu.VMEM((1, n_obs), jnp.int32),
            pltpu.VMEM((1, n_obs), jnp.int32),
            pltpu.VMEM((1, n_obs), jnp.int32),
            pltpu.VMEM((1, n_obs), F32),
            pltpu.VMEM((n_mem, own, part_rows), BF16),
            pltpu.VMEM((n_obs, rows), BF16),
            pltpu.VMEM((n_mem, P_SIZE, part_rows), BF16),
            pltpu.VMEM((n_mem, P_SIZE, part_rows), BF16),
            pltpu.VMEM((n_obs, P_SIZE), F32),
            pltpu.VMEM((n_obs, P_SIZE), F32),
            pltpu.VMEM((n_obs, P_SIZE), F32),
            pltpu.VMEM((n_obs, P_SIZE), F32),
            pltpu.VMEM((P_SIZE, 2 * P_SIZE + M), F32),
            pltpu.VMEM((P_SIZE, P_SIZE), F32),
            pltpu.VMEM((P_SIZE, M), F32),
            pltpu.VMEM((M, P_SIZE), BF16),
            pltpu.VMEM((BATCHES, owners, chunk, own), F32),
            pltpu.VMEM((BATCHES, n, chunk, own), F32),
            pltpu.VMEM((BATCHES, n_mem, owners, chunk, own), F32),
            pltpu.VMEM((c_owners, c_chunk, P_SIZE), F32),
            pltpu.VMEM((total, c_chunk, P_SIZE), F32),
            pltpu.VMEM((c_owners, c_chunk, P_SIZE), F32),
            pltpu.SemaphoreType.DMA((6,)),
            pltpu.SemaphoreType.DMA((n_mem,)),
            pltpu.SemaphoreType.DMA((n_mem,)),
            pltpu.SemaphoreType.DMA((BATCHES, n_mem)),
            pltpu.SemaphoreType.DMA((BATCHES, n_mem)),
            pltpu.SemaphoreType.DMA((BATCHES, owners)),
            pltpu.SemaphoreType.DMA((BATCHES, n)),
            pltpu.SemaphoreType.DMA((c_owners,)),
            pltpu.SemaphoreType.DMA((total,)),
            pltpu.SemaphoreType.DMA((BATCHES, total)),
            pltpu.SemaphoreType.DMA((BATCHES, n_mem, owners)),
            pltpu.SemaphoreType.DMA((total,)),
            pltpu.SemaphoreType.DMA((1, c_owners)),
        ],
        compiler_params=pltpu.CompilerParams(
            collective_id=0, has_side_effects=True, vmem_limit_bytes=40 * 1024 * 1024
        ),
    )(
        state,
        centers[None, :],
        half_width[None, :],
        radius[None, :],
        order[None, :],
        obs_var[None, :],
    )


def solution(mesh):
    shape = (mesh.shape["slab"], mesh.shape["mem"], mesh.shape["sub"])
    placed = (P("mem", ("grp", "slab", "sub")), P("grp"), P("grp"), P("grp"), P("grp"), P("grp"))
    return jax.shard_map(
        functools.partial(on_device, shape),
        mesh=mesh,
        in_specs=placed,
        out_specs=P("mem", ("grp", "slab", "sub")),
        check_vma=False,
    )
```

profile of v0, /device:TPU:0, one launch (start us, length us, event | category | flops | bytes accessed | tf_op | source)
XLA Modules:
  0.0 37.9 jit_solution(2183603980142455138)
XLA Ops:
  0.0 0.0 copy-start.4
  0.0 0.0 copy-start.5
  0.0 0.0 copy-start.2
  0.0 0.0 copy-start.3
  0.0 0.0 copy-start.1
  0.0 0.7 %copy-done.4 = s32[256]{0:T(256)S(1)} copy-done((s32[256]{0:T(256)S(1)}, s32[256]{0:T(256)}, u32[]{:S(2)}) %copy-start.4) | copy-done | bytes 1048
  0.7 0.0 copy-done.5
  0.7 0.0 copy-done.2
  0.7 0.0 copy-done.3
  0.7 0.0 copy-done.1
  0.7 0.0 copy-start
  0.7 1.0 %copy-done = bf16[128,2048]{1,0:T(8,128)(2,1)S(1)} copy-done((bf16[128,2048]{1,0:T(8,128)(2,1)S(1)}, bf16[128,2048]{1,0:T(8,128)(2,1)}, u32[]{:S(2)}) %copy-start) | copy-done | bytes 524312
  1.8 35.3 %shard_map.64 = bf16[128,2048]{1,0:T(8,128)(2,1)S(1)} custom-call(bf16[128,2048]{1,0:T(8,128)(2,1)S(1)} %copy-done, s32[1,256]{1,0:T(1,128)S(1)} %bitcast.5, s32[1,256]{1,0:T(1,128)S(1)} %bitcast.6, s32[1,256]{1,0:T(1,128)S(1)} %bitcast.7, s32[1,256]{1,0:T(1,128)S(1)} %bitcast.8, f32[1,256]{1,0:T(1,128)S(1)} %bitcast.9), custom_call_target="tpu_custom_call" | custom-call | tf_op jit(solution)/shard_map/pallas_call | solution.py:448
  37.1 0.8 %copy.8 = bf16[128,2048]{1,0:T(8,128)(2,1)} copy(bf16[128,2048]{1,0:T(8,128)(2,1)S(1)} %shard_map.64) | data formatting | bytes 1048576
Async XLA Ops:
  0.0 0.7 %copy-start.4 = (s32[256]{0:T(256)S(1)}, s32[256]{0:T(256)}, u32[]{:S(2)}) copy-start(s32[256]{0:T(256)} %param.10) | copy-start | bytes 3076
  0.0 0.7 %copy-start.5 = (f32[256]{0:T(256)S(1)}, f32[256]{0:T(256)}, u32[]{:S(2)}) copy-start(f32[256]{0:T(256)} %param.11) | copy-start | bytes 3076
  0.0 0.7 %copy-start.2 = (s32[256]{0:T(256)S(1)}, s32[256]{0:T(256)}, u32[]{:S(2)}) copy-start(s32[256]{0:T(256)} %param.8) | copy-start | bytes 3076
  0.0 0.7 %copy-start.3 = (s32[256]{0:T(256)S(1)}, s32[256]{0:T(256)}, u32[]{:S(2)}) copy-start(s32[256]{0:T(256)} %param.9) | copy-start | bytes 3076
  0.0 0.7 %copy-start.1 = (s32[256]{0:T(256)S(1)}, s32[256]{0:T(256)}, u32[]{:S(2)}) copy-start(s32[256]{0:T(256)} %param.7) | copy-start | bytes 3076
  0.7 1.0 %copy-start = (bf16[128,2048]{1,0:T(8,128)(2,1)S(1)}, bf16[128,2048]{1,0:T(8,128)(2,1)}, u32[]{:S(2)}) copy-start(bf16[128,2048]{1,0:T(8,128)(2,1)} %state_hbm.1) | copy-start | bytes 1572868
where the time goes:
time: 38 us; the launch traced here: 37.9 us
  Pallas kernels  35.3 us (93%)
  local copies, waits for them, and re-layouts  2.57 us (7%)
    pallas_call x1, Pallas kernels, on_device(): pl.pallas_call(functools.partial(kernel, shape), out_shape=jax.ShapeDtype...  35.3 us
    unnamed x13, local copies, waits for them, and re-layouts  2.57 us

commit v1 on v0

v1 whole, which is shorter than its diff:
```python
import functools
import math

import jax
import jax.numpy as jnp
from jax import lax
from jax.experimental import pallas as pl
from jax.experimental.pallas import tpu as pltpu
from jax.sharding import PartitionSpec as P

M = 256
P_SIZE = 128
BATCHES = 2
BLOCK = 16
SPLIT = 4

FLOOR = math.exp(-2.0)
F32 = jnp.float32
BF16 = jnp.bfloat16
HIGH = lax.Precision.HIGHEST
LAST = (((1,), (1,)), ((), ()))
FIRST = (((0,), (0,)), ((), ()))


def each(start, stop, body):
    if stop - start <= 16:
        for i in range(start, stop):
            body(i)
    else:

        def step(i, carry):
            body(i)
            return carry

        lax.fori_loop(start, stop, step, 0)


def split3(x):
    high = x.astype(BF16)
    rest = x - high.astype(F32)
    mid = rest.astype(BF16)
    low = (rest - mid.astype(F32)).astype(BF16)
    return high, mid, low


def sweep(work, inv, solved, root, first=0, last=P_SIZE // BLOCK, beside=None):
    b = BLOCK
    width = work.shape[1] // P_SIZE

    def step(k, carry):
        r0 = pl.multiple_of(k * b, b)
        parts = [work[pl.ds(r0, b), g * P_SIZE : (g + 1) * P_SIZE] for g in range(width)]
        roots = root[pl.ds(r0, b), :]
        rolled = pltpu.roll(parts[0], lax.rem(P_SIZE - r0, P_SIZE), 1)
        cols = [jnp.broadcast_to(rolled[:, j : j + 1], (b, P_SIZE)) for j in range(b)]
        row_id = lax.broadcasted_iota(jnp.int32, (b, P_SIZE), 0)
        for j in range(b):
            pivot = cols[j][j : j + 1, :]
            scale = lax.rsqrt(pivot)
            scale_m = 1.0 / (pivot * scale + roots[j : j + 1, :])
            column = jnp.where(row_id > j, cols[j] * scale, 0.0)
            for i in range(j + 1, b):
                cols[i] = cols[i] - column * column[i : i + 1, :]
            for g in range(width):
                row = parts[g][j : j + 1, :] * (scale if g < 2 else scale_m)
                parts[g] = jnp.where(row_id == j, row, parts[g] - column * row)
        inv[pl.ds(r0, b), :] = parts[1]
        for g in range(2, width):
            solved[pl.ds(r0, b), (g - 2) * P_SIZE : (g - 1) * P_SIZE] = parts[g]
        pieces = [split3(x) for x in parts]
        h, m, l = pieces[0]
        left = jnp.concatenate([h, h, m, h, m, l], axis=0)
        h, m, l = (jnp.concatenate([x[n] for x in pieces], axis=1) for n in range(3))
        right = jnp.concatenate([h, m, h, l, m, h], axis=0)
        work[...] -= lax.dot_general(left, right, FIRST, preferred_element_type=F32)
        if beside is not None:
            beside(k)
        return carry

    lax.fori_loop(first, last, step, 0)


def kernel(
    shape,
    state_hbm, cen_hbm, half_hbm, rad_hbm, order_hbm, var_hbm,
    out,
    ints, var,
    e_all, foot, tap, col_c, col_r, var_b, root_b, work, inv, solved, wts, p1, p1_b,
    part, rs, ag, cpart, crs, cag, sizes,
    in_s, e_s, x_s,
):
    n_slab, n_mem, n_sub = shape
    n = n_slab * n_sub
    total = n * n_mem
    own, rows = state_hbm.shape
    part_rows = rows // n_mem

    mi = lax.axis_index("mem")
    me = lax.axis_index("slab") * n_sub + lax.axis_index("sub")

    def peer(red, mem):
        return {"slab": lax.div(red, n_sub), "sub": lax.rem(red, n_sub), "mem": mem}

    def peer_of(off):
        red = lax.rem(me + lax.rem(off, n), n)
        mem = lax.rem(mi + lax.div(off, n), n_mem)
        return red, mem

    def remote(src, dst, send, recv, device):
        return pltpu.make_async_remote_copy(
            src_ref=src, dst_ref=dst, send_sem=send, recv_sem=recv,
            device_id=device, device_id_type=pl.DeviceIdType.MESH,
        )

    def wait_sent(ref, sem):
        remote(ref, ref, sem, sem, peer(me, mi)).wait_send()

    def wait_recv(ref, sem):
        remote(ref, ref, sem, sem, peer(me, mi)).wait_recv()

    small = [
        pltpu.make_async_copy(a, ints.at[i], in_s.at[0])
        for i, a in enumerate((cen_hbm, half_hbm, rad_hbm, order_hbm))
    ]
    var_copy = pltpu.make_async_copy(var_hbm, var, in_s.at[1])
    state_copy = pltpu.make_async_copy(state_hbm, e_all.at[mi], in_s.at[2])
    for copy in small:
        copy.start()
    var_copy.start()
    state_copy.start()

    barrier = pltpu.get_barrier_semaphore()

    def greet(off):
        red, mem = peer_of(off)
        pl.semaphore_signal(
            barrier, inc=1, device_id=peer(red, mem), device_id_type=pl.DeviceIdType.MESH
        )

    each(1, total, greet)
    pltpu.make_async_copy(ints, ints, in_s.at[0]).wait()
    var_copy.wait()

    n_obs = BATCHES * P_SIZE
    picked = jnp.broadcast_to(ints[3].astype(F32), (P_SIZE, n_obs)).T.astype(jnp.int32)
    lane = lax.broadcasted_iota(jnp.int32, (n_obs, P_SIZE), 1)
    masks = [picked == lane + h * P_SIZE for h in range(BATCHES)]

    def pick(ref):
        value = ref[...].astype(F32)
        chosen = 0.0
        for h in range(BATCHES):
            chosen = chosen + jnp.where(masks[h], value[:, h * P_SIZE : (h + 1) * P_SIZE], 0.0)
        return jnp.sum(chosen, axis=1, keepdims=True)

    center = pick(ints.at[0]) - (me * rows).astype(F32)
    width = pick(ints.at[1])
    variance = pick(var)
    col_c[...] = jnp.broadcast_to(center, (n_obs, P_SIZE))
    col_r[...] = jnp.broadcast_to(1.0 / pick(ints.at[2]), (n_obs, P_SIZE))
    var_b[...] = jnp.broadcast_to(variance, (n_obs, P_SIZE))
    root_b[...] = jnp.broadcast_to(jnp.sqrt(variance), (n_obs, P_SIZE))
    steep = -2.0 / (width * width)
    height = 1.0 / jnp.sqrt(width)

    def rows_of(mem):
        return pl.ds(pl.multiple_of(mem * part_rows, part_rows), part_rows)

    my_rows = rows_of(mi)

    def e_copy(off, q):
        to = lax.rem(mi + off, n_mem)
        at = rows_of(lax.rem(to + q, n_mem))
        k = 0 if q == 0 else 2
        return remote(
            state_hbm.at[:, at], e_all.at[mi, :, at], e_s.at[k], e_s.at[k + 1], peer(me, to)
        )

    def project(b):
        lo = b * P_SIZE

        def foot_tile(t, carry):
            at = pl.multiple_of(t * 256, 256)
            row = lax.broadcasted_iota(jnp.int32, (P_SIZE, 256), 1) + at
            distance = row.astype(F32) - center[lo : lo + P_SIZE]
            shape_f = jnp.exp(distance * distance * steep[lo : lo + P_SIZE]) - FLOOR
            shape_f = jnp.maximum(shape_f, 0.0) * height[lo : lo + P_SIZE]
            foot[lo : lo + P_SIZE, pl.ds(at, 256)] = shape_f.astype(BF16)
            return carry

        lax.fori_loop(0, rows // 256, foot_tile, 0)
        if b == 0:
            state_copy.wait()
        sums = lax.dot_general(
            foot[lo : lo + P_SIZE, :], e_all[mi], LAST, preferred_element_type=F32
        )
        part[b] = sums.reshape(part.shape[1:])

    class Sum:
        def __init__(self, size, index, device, source, target, result, everyone, sem, flat, span):
            self.size, self.index, self.device = size, index, device
            self.source, self.target, self.result, self.everyone = source, target, result, everyone
            self.sem, self.flat, self.span = sem, flat, span
            self.owners = source.shape[0]
            self.stride = size // self.owners
            self.mine = lax.div(index, self.stride)

        def if_owner(self, body, owner=True):
            if self.stride == 1:
                if owner:
                    body()
            else:
                pl.when((lax.rem(self.index, self.stride) == 0) == owner)(body)

        def out_copy(self, off):
            o = lax.rem(self.mine + off, self.owners)
            return remote(
                self.source.at[o], self.target.at[self.index],
                self.sem.at[0], self.sem.at[1], self.device(o * self.stride),
            )

        def start(self):
            each(1, self.owners, lambda off: self.out_copy(off).start())
            self.if_owner(lambda: self.out_copy(0).start(), False)

        def gather_copy(self, off):
            block = self.result(mi, self.mine)
            return remote(
                block, block, self.sem.at[2], self.sem.at[3], peer(*peer_of(off))
            )

        def finish(self):
            def body():
                wait_recv(self.target.at[pl.ds(0, self.size - 1)], self.sem.at[1])
                block = self.result(mi, self.mine)
                if self.size <= 16:
                    value = self.source[self.mine]
                    for off in range(1, self.size):
                        value = value + self.target[lax.rem(self.index + off, self.size)]
                    block[...] = value
                else:
                    block[...] = self.source[self.mine]

                    def add(off):
                        block[...] += self.target[lax.rem(self.index + off, self.size)]

                    each(1, self.size, add)
                each(1, total, lambda off: self.gather_copy(off).start())

            self.if_owner(body)

        def gather(self):
            count = (n_mem if self.everyone else 1) * self.owners
            self.if_owner(lambda: wait_recv(self.flat.at[pl.ds(0, count - 1)], self.sem.at[3]))
            self.if_owner(lambda: wait_recv(self.flat.at[pl.ds(0, count)], self.sem.at[3]), False)

        def sent(self):
            self.if_owner(
                lambda: wait_sent(self.source.at[pl.ds(0, self.owners - 1)], self.sem.at[0])
            )
            self.if_owner(lambda: wait_sent(self.source, self.sem.at[0]), False)
            self.if_owner(lambda: wait_sent(self.span.at[pl.ds(0, total - 1)], self.sem.at[2]))

    owners = part.shape[1]
    projections = [
        Sum(
            n, me, lambda i: peer(i, mi), part.at[b], rs.at[b],
            lambda mem, o, b=b: ag.at[b, mem * owners + o], True, x_s.at[b], ag.at[b], sizes,
        )
        for b in range(BATCHES)
    ]
    changes = Sum(
        total, mi * n + me, lambda i: peer(lax.rem(i, n), lax.div(i, n)), cpart, crs,
        lambda mem, o: cag.at[o], False, x_s.at[BATCHES], cag, crs,
    )
    project(0)
    pl.semaphore_wait(barrier, total - 1)
    projections[0].start()
    each(1, n_mem, lambda off: e_copy(off, 0).start())
    project(1)
    projections[1].start()
    projections[0].finish()
    for q in range(1, n_mem):
        each(1, n_mem, lambda off: e_copy(off, q).start())

    def slot(b, s):
        return ag[b, s * owners : (s + 1) * owners].reshape(P_SIZE, own)

    def load_work(columns, extra, b):
        cov = 0.0
        for s in range(n_mem):
            cov = cov + lax.dot_general(
                columns[s], columns[s], LAST, precision=HIGH, preferred_element_type=F32
            )
        r = lax.broadcasted_iota(jnp.int32, (P_SIZE, P_SIZE), 0)
        eye = r == lax.broadcasted_iota(jnp.int32, (P_SIZE, P_SIZE), 1)
        v = var_b[b * P_SIZE : (b + 1) * P_SIZE, :]
        work[:, :P_SIZE] = cov * (1.0 / (M - 1)) + jnp.where(eye, v, 0.0)
        work[:, P_SIZE : 2 * P_SIZE] = jnp.where(eye, 1.0, 0.0)
        lo = 2 * P_SIZE
        for x in extra:
            work[:, lo : lo + own] = x
            lo += own

    def taper(b, first, count):
        lo = b * P_SIZE
        row = lax.broadcasted_iota(jnp.int32, (P_SIZE, count), 1) + first
        c = jnp.concatenate([col_c[lo : lo + P_SIZE, :]] * (count // P_SIZE), axis=1)
        r = jnp.concatenate([col_r[lo : lo + P_SIZE, :]] * (count // P_SIZE), axis=1)
        near = jnp.maximum(1.0 - jnp.abs(row.astype(F32) - c) * r, 0.0)
        return near * near * (1.0 / (M - 1))

    projections[0].gather()
    first = [slot(0, s) for s in range(n_mem)]
    first_b = [x.astype(BF16) for x in first]

    def cross(which):
        mem = lax.rem(mi + which, n_mem)
        at = rows_of(mem)
        product = 0.0
        for s in range(n_mem):
            product = product + jnp.dot(first_b[s], e_all[s, :, at], preferred_element_type=F32)
        value = (taper(0, mem * part_rows, part_rows) * product).astype(BF16)
        tap[:, at] = value
        return value

    wait_recv(e_all.at[pl.ds(0, n_mem - 1), :, pl.ds(0, part_rows)], e_s.at[1])

    change = lax.dot_general(
        foot[P_SIZE : 2 * P_SIZE, my_rows], cross(0), LAST, preferred_element_type=F32
    )
    cpart[...] = change.reshape(cpart.shape)
    changes.start()
    projections[1].finish()

    load_work(first, first, 0)
    root_0 = root_b.at[pl.ds(0, P_SIZE)]
    sweep(work, inv, solved, root_0, 0, SPLIT)
    changes.finish()
    sweep(work, inv, solved, root_0, SPLIT)

    def weights(count):
        return lax.dot_general(
            solved[:, :count], inv[...], FIRST, precision=HIGH, preferred_element_type=F32
        ).astype(BF16)

    wts[...] = weights(M)

    wait_recv(
        e_all.at[pl.ds(0, n_mem - 1), :, pl.ds(0, (n_mem - 1) * part_rows)], e_s.at[3]
    )
    for q in range(1, n_mem):
        cross(q)
    def update(s):
        moved = jnp.dot(wts[s * own : (s + 1) * own, :], tap[...], preferred_element_type=F32)
        e_all[s] = (e_all[s].astype(F32) - moved).astype(BF16)

    for s in range(n_mem):
        update(s)

    projections[1].gather()
    changes.gather()
    c_full = jnp.concatenate(split3(cag[...].reshape(P_SIZE, P_SIZE)), axis=0)
    moved = lax.dot_general(c_full, wts[...], LAST, preferred_element_type=F32)
    moved = moved[:P_SIZE] + (moved[P_SIZE : 2 * P_SIZE] + moved[2 * P_SIZE :])
    second = []
    for s in range(n_mem):
        value = slot(1, s) - moved[:, s * own : (s + 1) * own]
        p1[s] = value
        p1_b[s] = value.astype(BF16)
        second.append(value)

    alone = own % P_SIZE == 0
    load_work(second, [p1[mi]] if alone else second, 1)

    def cross1(k):
        size = rows * BLOCK // P_SIZE
        at = pl.ds(pl.multiple_of(k * size, size), size)
        product = 0.0
        for s in range(n_mem):
            product = product + jnp.dot(p1_b[s], e_all[s, :, at], preferred_element_type=F32)
        tap[:, at] = (taper(1, k * size, size) * product).astype(BF16)

    used = 2 * P_SIZE + (own if alone else M)
    sweep(
        work.at[:, pl.ds(0, used)], inv, solved, root_b.at[pl.ds(P_SIZE, P_SIZE)], beside=cross1
    )
    if alone:
        own_w = weights(own)
    else:
        wts[...] = weights(M)
        own_w = wts[pl.ds(pl.multiple_of(mi * own, own), own), :]

    moved = jnp.dot(own_w, tap[...], preferred_element_type=F32)
    out[...] = (e_all[mi].astype(F32) - moved).astype(BF16)

    wait_sent(e_all.at[pl.ds(0, n_mem - 1), :, pl.ds(0, part_rows)], e_s.at[0])
    wait_sent(e_all.at[pl.ds(0, n_mem - 1), :, pl.ds(0, (n_mem - 1) * part_rows)], e_s.at[2])
    for x in projections + [changes]:
        x.sent()


def on_device(shape, state, centers, half_width, radius, order, obs_var):
    n_slab, n_mem, n_sub = shape
    own, rows = state.shape
    n = n_slab * n_sub
    total = n * n_mem
    owners = min(n, 8)
    chunk = P_SIZE // owners
    c_owners = min(total, 16)
    c_chunk = P_SIZE // c_owners
    n_obs = BATCHES * P_SIZE
    operands = (state,) + tuple(
        x[None, :] for x in (centers, half_width, radius, order, obs_var)
    )
    hbm = pl.BlockSpec(memory_space=pltpu.HBM)
    vmem = pl.BlockSpec(memory_space=pltpu.VMEM)
    return pl.pallas_call(
        functools.partial(kernel, shape),
        out_shape=pltpu.VMEM((own, rows), BF16),
        in_specs=[hbm] * 6,
        out_specs=vmem,
        scratch_shapes=[
            pltpu.VMEM((4, 1, n_obs), jnp.int32),
            pltpu.VMEM((1, n_obs), F32),
            pltpu.VMEM((n_mem, own, rows), BF16),
            pltpu.VMEM((n_obs, rows), BF16),
            pltpu.VMEM((P_SIZE, rows), BF16),
            pltpu.VMEM((n_obs, P_SIZE), F32),
            pltpu.VMEM((n_obs, P_SIZE), F32),
            pltpu.VMEM((n_obs, P_SIZE), F32),
            pltpu.VMEM((n_obs, P_SIZE), F32),
            pltpu.VMEM((P_SIZE, 2 * P_SIZE + M), F32),
            pltpu.VMEM((P_SIZE, P_SIZE), F32),
            pltpu.VMEM((P_SIZE, M), F32),
            pltpu.VMEM((M, P_SIZE), BF16),
            pltpu.VMEM((n_mem, P_SIZE, own), F32),
            pltpu.VMEM((n_mem, P_SIZE, own), BF16),
            pltpu.VMEM((BATCHES, owners, chunk, own), F32),
            pltpu.VMEM((BATCHES, n, chunk, own), F32),
            pltpu.VMEM((BATCHES, n_mem * owners, chunk, own), F32),
            pltpu.VMEM((c_owners, c_chunk, P_SIZE), F32),
            pltpu.VMEM((total, c_chunk, P_SIZE), F32),
            pltpu.VMEM((c_owners, c_chunk, P_SIZE), F32),
            pltpu.VMEM((total, chunk, own), F32),
            pltpu.SemaphoreType.DMA((3,)),
            pltpu.SemaphoreType.DMA((4,)),
            pltpu.SemaphoreType.DMA((BATCHES + 1, 4)),
        ],
        compiler_params=pltpu.CompilerParams(
            collective_id=0, has_side_effects=True, vmem_limit_bytes=40 * 1024 * 1024
        ),
    )(*(pltpu.with_memory_space_constraint(x, pltpu.HBM) for x in operands))


def solution(mesh):
    shape = (mesh.shape["slab"], mesh.shape["mem"], mesh.shape["sub"])
    placed = (P("mem", ("grp", "slab", "sub")), P("grp"), P("grp"), P("grp"), P("grp"), P("grp"))
    return jax.shard_map(
        functools.partial(on_device, shape),
        mesh=mesh,
        in_specs=placed,
        out_specs=P("mem", ("grp", "slab", "sub")),
        check_vma=False,
    )
```

time: 38 us -> 32.9 us (0.87)
  Pallas kernels: 35.3 us -> 32 us
  local copies, waits for them, and re-layouts: 2.57 us -> 0.8 us
    pallas_call x1, Pallas kernels: 35.3 us -> 32 us  [on_device(): pl.pallas_call(functools.partial(kernel, shape), out_shape=pltpu.VMEM((ow...]
    unnamed x13 -> x1, local copies, waits for them, and re-layouts: 2.57 us -> 0.8 us
where the time goes in v1:
time: 32.9 us; the launch traced here: 32.8 us
  Pallas kernels  32 us (97%)
  local copies, waits for them, and re-layouts  0.8 us (2%)
    pallas_call x1, Pallas kernels, on_device(): pl.pallas_call(functools.partial(kernel, shape), out_shape=pltpu.VMEM((ow...  32 us
    unnamed x1, local copies, waits for them, and re-layouts  0.8 us

profile of v1, /device:TPU:0, one launch (start us, length us, event | category | flops | bytes accessed | tf_op | source)
XLA Modules:
  0.0 32.8 jit_solution(10427724227006648689)
XLA Ops:
  0.0 32.0 %shard_map.64 = bf16[128,2048]{1,0:T(8,128)(2,1)S(1)} custom-call(bf16[128,2048]{1,0:T(8,128)(2,1)} %state_hbm.1, s32[1,256]{1,0:T(1,128)} %bitcast.5, s32[1,256]{1,0:T(1,128)} %bitcast.6, s32[1,256]{1,0:T(1,128)} %bitcast.7, s32[1,256]{1,0:T(1,128)} %bitcast.8, f32[1,256]{1,0:T(1,128)} %bitcast.9), custom_call_target="tpu_custom_call" | custom-call | tf_op jit(solution)/shard_map/pallas_call | solution.py:418
  32.0 0.8 %copy.8 = bf16[128,2048]{1,0:T(8,128)(2,1)} copy(bf16[128,2048]{1,0:T(8,128)(2,1)S(1)} %shard_map.64) | data formatting | bytes 1048576

commit v2 on v1

--- a/solution.py
+++ b/solution.py
@@ -11,8 +11,7 @@
 M = 256
 P_SIZE = 128
 BATCHES = 2
-BLOCK = 16
-SPLIT = 4
+BLOCK = 32
 
 FLOOR = math.exp(-2.0)
 F32 = jnp.float32
@@ -43,41 +42,77 @@
     return high, mid, low
 
 
-def sweep(work, inv, solved, root, first=0, last=P_SIZE // BLOCK, beside=None):
+def block(work, inv, solved, root, k):
     b = BLOCK
+    size = b // 8
     width = work.shape[1] // P_SIZE
-
-    def step(k, carry):
-        r0 = pl.multiple_of(k * b, b)
-        parts = [work[pl.ds(r0, b), g * P_SIZE : (g + 1) * P_SIZE] for g in range(width)]
-        roots = root[pl.ds(r0, b), :]
-        rolled = pltpu.roll(parts[0], lax.rem(P_SIZE - r0, P_SIZE), 1)
-        cols = [jnp.broadcast_to(rolled[:, j : j + 1], (b, P_SIZE)) for j in range(b)]
-        row_id = lax.broadcasted_iota(jnp.int32, (b, P_SIZE), 0)
-        for j in range(b):
-            pivot = cols[j][j : j + 1, :]
-            scale = lax.rsqrt(pivot)
-            scale_m = 1.0 / (pivot * scale + roots[j : j + 1, :])
-            column = jnp.where(row_id > j, cols[j] * scale, 0.0)
-            for i in range(j + 1, b):
-                cols[i] = cols[i] - column * column[i : i + 1, :]
-            for g in range(width):
-                row = parts[g][j : j + 1, :] * (scale if g < 2 else scale_m)
-                parts[g] = jnp.where(row_id == j, row, parts[g] - column * row)
-        inv[pl.ds(r0, b), :] = parts[1]
-        for g in range(2, width):
-            solved[pl.ds(r0, b), (g - 2) * P_SIZE : (g - 1) * P_SIZE] = parts[g]
-        pieces = [split3(x) for x in parts]
-        h, m, l = pieces[0]
-        left = jnp.concatenate([h, h, m, h, m, l], axis=0)
-        h, m, l = (jnp.concatenate([x[n] for x in pieces], axis=1) for n in range(3))
-        right = jnp.concatenate([h, m, h, l, m, h], axis=0)
-        work[...] -= lax.dot_general(left, right, FIRST, preferred_element_type=F32)
-        if beside is not None:
-            beside(k)
-        return carry
-
-    lax.fori_loop(first, last, step, 0)
+    r0 = k * b
+
+    def at(v):
+        return pl.ds(r0 + 8 * v, 8)
+
+    def spread(x, i):
+        return jnp.broadcast_to(x[i : i + 1, :], (8, P_SIZE))
+
+    row = lax.broadcasted_iota(jnp.int32, (8, P_SIZE), 0)
+    lane = lax.broadcasted_iota(jnp.int32, (8, P_SIZE), 1) - r0
+    parts = [
+        [work[at(v), g * P_SIZE : (g + 1) * P_SIZE] for v in range(size)] for g in range(width)
+    ]
+    roots = [root[at(v), :] for v in range(size)]
+    cols = [
+        {
+            v: jnp.broadcast_to(parts[0][v][:, r0 + j : r0 + j + 1], (8, P_SIZE))
+            for v in range(j // 8, size)
+        }
+        for j in range(b)
+    ]
+    inside = (lane >= 0) & (lane < b)
+    for v in range(size):
+        unit = jnp.where(lane == row + 8 * v, 1.0, 0.0)
+        parts[0][v] = jnp.where(inside, unit, parts[0][v])
+    pivots = [jnp.ones((8, P_SIZE), F32)] * size
+    for j in range(b):
+        top, jj = j // 8, j % 8
+        column = cols[j]
+        pivot = spread(column[top], jj)
+        scale = lax.rsqrt(pivot)
+        plain = scale * scale
+        mixed = scale / (pivot * scale + spread(roots[top], jj))
+        pivots[top] = jnp.where(row == jj, column[top], pivots[top])
+        below = dict(column)
+        below[top] = jnp.where(row > jj, column[top], 0.0)
+        first = {v: x * plain for v, x in below.items()}
+        other = {v: x * mixed for v, x in below.items()}
+        for i in range(j + 1, b):
+            s = spread(column[i // 8], i % 8)
+            for v in range(i // 8, size):
+                cols[i][v] = cols[i][v] - first[v] * s
+        for g in range(width):
+            line = spread(parts[g][top], jj)
+            for v in range(top, size):
+                parts[g][v] = parts[g][v] - (other if g else first)[v] * line
+    for v in range(size):
+        scale = lax.rsqrt(pivots[v])
+        mixed = 1.0 / (pivots[v] * scale + roots[v])
+        for g in range(width):
+            parts[g][v] = parts[g][v] * (mixed if g else scale)
+        inv[at(v), :] = jnp.where(lane < b, parts[0][v], 0.0)
+        for g in range(1, width):
+            solved[at(v), (g - 1) * P_SIZE : g * P_SIZE] = parts[g][v]
+    lo = r0 + b
+    if lo == P_SIZE:
+        return
+    pieces = [split3(jnp.concatenate(x, axis=0)) for x in parts]
+    h, m, l = pieces[0]
+    left = jnp.concatenate([h, h, m, h, m, l], axis=0)
+    h, m, l = (jnp.concatenate([x[n] for x in pieces], axis=1) for n in range(3))
+    right = jnp.concatenate([h, m, h, l, m, h], axis=0)
+    change = lax.dot_general(left, right, FIRST, preferred_element_type=F32)[lo:]
+    lane = lax.broadcasted_iota(jnp.int32, (P_SIZE - lo, P_SIZE), 1) - r0
+    old = jnp.where((lane >= 0) & (lane < b), 0.0, work[lo:, :P_SIZE])
+    work[lo:, :P_SIZE] = old - change[:, :P_SIZE]
+    work[lo:, P_SIZE:] -= change[:, P_SIZE:]
 
 
 def kernel(
@@ -86,7 +121,7 @@
     out,
     ints, var,
     e_all, foot, tap, col_c, col_r, var_b, root_b, work, inv, solved, wts, p1, p1_b,
-    part, rs, ag, cpart, crs, cag, sizes,
+    part, rs, ag, ag_b, cpart, crs, cag, sizes, sizes_b,
     in_s, e_s, x_s,
 ):
     n_slab, n_mem, n_sub = shape
@@ -168,13 +203,30 @@
 
     my_rows = rows_of(mi)
 
-    def e_copy(off, q):
+    half_rows = part_rows // 2
+
+    def half_of(mem, c):
+        return pl.ds(pl.multiple_of(mem * part_rows + c * half_rows, half_rows), half_rows)
+
+    def e_copy(off):
         to = lax.rem(mi + off, n_mem)
-        at = rows_of(lax.rem(to + q, n_mem))
-        k = 0 if q == 0 else 2
+        at = rows_of(to)
         return remote(
-            state_hbm.at[:, at], e_all.at[mi, :, at], e_s.at[k], e_s.at[k + 1], peer(me, to)
-        )
+            state_hbm.at[:, at], e_all.at[mi, :, at], e_s.at[0], e_s.at[1], peer(me, to)
+        )
+
+    def rest_copy(off, c):
+        to = lax.rem(mi + lax.rem(off, n_mem - 1) + 1, n_mem)
+        at = half_of(lax.rem(to + lax.div(off, n_mem - 1) + 1, n_mem), c)
+        return remote(
+            state_hbm.at[:, at], e_all.at[mi, :, at], e_s.at[2 + 2 * c], e_s.at[3 + 2 * c],
+            peer(me, to),
+        )
+
+    def send_rest(c):
+        each(0, (n_mem - 1) * (n_mem - 1), lambda off: rest_copy(off, c).start())
+
+    rest = e_all.at[pl.ds(0, n_mem - 1), :, pl.ds(0, (n_mem - 1) * half_rows)]
 
     def project(b):
         lo = b * P_SIZE
@@ -197,10 +249,10 @@
         part[b] = sums.reshape(part.shape[1:])
 
     class Sum:
-        def __init__(self, size, index, device, source, target, result, everyone, sem, flat, span):
+        def __init__(self, size, index, device, source, target, result, everyone, sem, flat, span, high=None):
             self.size, self.index, self.device = size, index, device
             self.source, self.target, self.result, self.everyone = source, target, result, everyone
-            self.sem, self.flat, self.span = sem, flat, span
+            self.sem, self.flat, self.span, self.high = sem, flat, span, high
             self.owners = source.shape[0]
             self.stride = size // self.owners
             self.mine = lax.div(index, self.stride)
@@ -227,6 +279,12 @@
             block = self.result(mi, self.mine)
             return remote(
                 block, block, self.sem.at[2], self.sem.at[3], peer(*peer_of(off))
+            )
+
+        def high_copy(self, off):
+            block = self.high.at[mi * self.owners + self.mine]
+            return remote(
+                block, block, self.sem.at[4], self.sem.at[5], peer(*peer_of(off))
             )
 
         def finish(self):
@@ -245,14 +303,24 @@
                         block[...] += self.target[lax.rem(self.index + off, self.size)]
 
                     each(1, self.size, add)
+                if self.high is not None:
+                    value = block[...]
+                    high = value.astype(BF16)
+                    self.high[mi * self.owners + self.mine] = high
+                    each(1, total, lambda off: self.high_copy(off).start())
+                    block[...] = value - high.astype(F32)
                 each(1, total, lambda off: self.gather_copy(off).start())
 
             self.if_owner(body)
 
-        def gather(self):
+        def gather(self, flat=None, sem=3):
+            flat = self.flat if flat is None else flat
             count = (n_mem if self.everyone else 1) * self.owners
-            self.if_owner(lambda: wait_recv(self.flat.at[pl.ds(0, count - 1)], self.sem.at[3]))
-            self.if_owner(lambda: wait_recv(self.flat.at[pl.ds(0, count)], self.sem.at[3]), False)
+            self.if_owner(lambda: wait_recv(flat.at[pl.ds(0, count - 1)], self.sem.at[sem]))
+            self.if_owner(lambda: wait_recv(flat.at[pl.ds(0, count)], self.sem.at[sem]), False)
+
+        def gather_high(self):
+            self.gather(self.high, 5)
 
         def sent(self):
             self.if_owner(
@@ -260,12 +328,15 @@
             )
             self.if_owner(lambda: wait_sent(self.source, self.sem.at[0]), False)
             self.if_owner(lambda: wait_sent(self.span.at[pl.ds(0, total - 1)], self.sem.at[2]))
+            if self.high is not None:
+                self.if_owner(lambda: wait_sent(sizes_b.at[pl.ds(0, total - 1)], self.sem.at[4]))
 
     owners = part.shape[1]
     projections = [
         Sum(
             n, me, lambda i: peer(i, mi), part.at[b], rs.at[b],
             lambda mem, o, b=b: ag.at[b, mem * owners + o], True, x_s.at[b], ag.at[b], sizes,
+            ag_b if b == 0 else None,
         )
         for b in range(BATCHES)
     ]
@@ -276,12 +347,11 @@
     project(0)
     pl.semaphore_wait(barrier, total - 1)
     projections[0].start()
-    each(1, n_mem, lambda off: e_copy(off, 0).start())
+    each(1, n_mem, lambda off: e_copy(off).start())
     project(1)
     projections[1].start()
     projections[0].finish()
-    for q in range(1, n_mem):
-        each(1, n_mem, lambda off: e_copy(off, q).start())
+    send_rest(0)
 
     def slot(b, s):
         return ag[b, s * owners : (s + 1) * owners].reshape(P_SIZE, own)
@@ -296,8 +366,7 @@
         eye = r == lax.broadcasted_iota(jnp.int32, (P_SIZE, P_SIZE), 1)
         v = var_b[b * P_SIZE : (b + 1) * P_SIZE, :]
         work[:, :P_SIZE] = cov * (1.0 / (M - 1)) + jnp.where(eye, v, 0.0)
-        work[:, P_SIZE : 2 * P_SIZE] = jnp.where(eye, 1.0, 0.0)
-        lo = 2 * P_SIZE
+        lo = P_SIZE
         for x in extra:
             work[:, lo : lo + own] = x
             lo += own
@@ -310,34 +379,45 @@
         near = jnp.maximum(1.0 - jnp.abs(row.astype(F32) - c) * r, 0.0)
         return near * near * (1.0 / (M - 1))
 
-    projections[0].gather()
-    first = [slot(0, s) for s in range(n_mem)]
-    first_b = [x.astype(BF16) for x in first]
-
-    def cross(which):
-        mem = lax.rem(mi + which, n_mem)
-        at = rows_of(mem)
+    projections[0].gather_high()
+    first_b = [ag_b[s * owners : (s + 1) * owners].reshape(P_SIZE, own) for s in range(n_mem)]
+
+    def cross(b, left, at, size):
         product = 0.0
         for s in range(n_mem):
-            product = product + jnp.dot(first_b[s], e_all[s, :, at], preferred_element_type=F32)
-        value = (taper(0, mem * part_rows, part_rows) * product).astype(BF16)
+            product = product + jnp.dot(left[s], e_all[s, :, at], preferred_element_type=F32)
+        value = (taper(b, at.start, size) * product).astype(BF16)
         tap[:, at] = value
         return value
 
+    def update(at):
+        for s in range(n_mem):
+            moved = jnp.dot(
+                wts[s * own : (s + 1) * own, :], tap[:, at], preferred_element_type=F32
+            )
+            e_all[s, :, at] = (e_all[s, :, at].astype(F32) - moved).astype(BF16)
+
     wait_recv(e_all.at[pl.ds(0, n_mem - 1), :, pl.ds(0, part_rows)], e_s.at[1])
 
     change = lax.dot_general(
-        foot[P_SIZE : 2 * P_SIZE, my_rows], cross(0), LAST, preferred_element_type=F32
+        foot[P_SIZE : 2 * P_SIZE, my_rows], cross(0, first_b, my_rows, part_rows),
+        LAST, preferred_element_type=F32,
     )
     cpart[...] = change.reshape(cpart.shape)
     changes.start()
     projections[1].finish()
 
+    projections[0].gather()
+    first = [first_b[s].astype(F32) + slot(0, s) for s in range(n_mem)]
     load_work(first, first, 0)
     root_0 = root_b.at[pl.ds(0, P_SIZE)]
-    sweep(work, inv, solved, root_0, 0, SPLIT)
+    blocks = P_SIZE // BLOCK
+    for k in range(blocks // 2):
+        block(work, inv, solved, root_0, k)
     changes.finish()
-    sweep(work, inv, solved, root_0, SPLIT)
+    send_rest(1)
+    for k in range(blocks // 2, blocks):
+        block(work, inv, solved, root_0, k)
 
     def weights(count):
         return lax.dot_general(
@@ -346,17 +426,14 @@
 
     wts[...] = weights(M)
 
-    wait_recv(
-        e_all.at[pl.ds(0, n_mem - 1), :, pl.ds(0, (n_mem - 1) * part_rows)], e_s.at[3]
-    )
-    for q in range(1, n_mem):
-        cross(q)
-    def update(s):
-        moved = jnp.dot(wts[s * own : (s + 1) * own, :], tap[...], preferred_element_type=F32)
-        e_all[s] = (e_all[s].astype(F32) - moved).astype(BF16)
-
-    for s in range(n_mem):
-        update(s)
+    def others(c):
+        return [half_of(lax.rem(mi + q, n_mem), c) for q in range(1, n_mem)]
+
+    update(my_rows)
+    wait_recv(rest, e_s.at[3])
+    for at in others(0):
+        cross(0, first_b, at, half_rows)
+        update(at)
 
     projections[1].gather()
     changes.gather()
@@ -373,18 +450,27 @@
     alone = own % P_SIZE == 0
     load_work(second, [p1[mi]] if alone else second, 1)
 
-    def cross1(k):
-        size = rows * BLOCK // P_SIZE
-        at = pl.ds(pl.multiple_of(k * size, size), size)
-        product = 0.0
-        for s in range(n_mem):
-            product = product + jnp.dot(p1_b[s], e_all[s, :, at], preferred_element_type=F32)
-        tap[:, at] = (taper(1, k * size, size) * product).astype(BF16)
-
-    used = 2 * P_SIZE + (own if alone else M)
-    sweep(
-        work.at[:, pl.ds(0, used)], inv, solved, root_b.at[pl.ds(P_SIZE, P_SIZE)], beside=cross1
-    )
+    def beside(k):
+        if k < 2:
+            tiles = [half_of(mi, k)]
+        elif k < 4:
+            tiles = others(k - 2)
+        else:
+            tiles = []
+        for at in tiles:
+            if k == 3:
+                cross(0, first_b, at, half_rows)
+                update(at)
+            cross(1, p1_b, at, half_rows)
+
+    used = P_SIZE + (own if alone else M)
+    for k in range(blocks):
+        if k == 3:
+            wait_recv(rest, e_s.at[5])
+        block(
+            work.at[:, pl.ds(0, used)], inv, solved, root_b.at[pl.ds(P_SIZE, P_SIZE)], k
+        )
+        beside(k)
     if alone:
         own_w = weights(own)
     else:
@@ -395,7 +481,8 @@
     out[...] = (e_all[mi].astype(F32) - moved).astype(BF16)
 
     wait_sent(e_all.at[pl.ds(0, n_mem - 1), :, pl.ds(0, part_rows)], e_s.at[0])
-    wait_sent(e_all.at[pl.ds(0, n_mem - 1), :, pl.ds(0, (n_mem - 1) * part_rows)], e_s.at[2])
+    wait_sent(rest, e_s.at[2])
+    wait_sent(rest, e_s.at[4])
     for x in projections + [changes]:
         x.sent()
 
@@ -430,7 +517,7 @@
             pltpu.VMEM((n_obs, P_SIZE), F32),
             pltpu.VMEM((n_obs, P_SIZE), F32),
             pltpu.VMEM((n_obs, P_SIZE), F32),
-            pltpu.VMEM((P_SIZE, 2 * P_SIZE + M), F32),
+            pltpu.VMEM((P_SIZE, P_SIZE + M), F32),
             pltpu.VMEM((P_SIZE, P_SIZE), F32),
             pltpu.VMEM((P_SIZE, M), F32),
             pltpu.VMEM((M, P_SIZE), BF16),
@@ -439,13 +526,15 @@
             pltpu.VMEM((BATCHES, owners, chunk, own), F32),
             pltpu.VMEM((BATCHES, n, chunk, own), F32),
             pltpu.VMEM((BATCHES, n_mem * owners, chunk, own), F32),
+            pltpu.VMEM((n_mem * owners, chunk, own), BF16),
             pltpu.VMEM((c_owners, c_chunk, P_SIZE), F32),
             pltpu.VMEM((total, c_chunk, P_SIZE), F32),
             pltpu.VMEM((c_owners, c_chunk, P_SIZE), F32),
             pltpu.VMEM((total, chunk, own), F32),
+            pltpu.VMEM((total, chunk, own), BF16),
             pltpu.SemaphoreType.DMA((3,)),
-            pltpu.SemaphoreType.DMA((4,)),
-            pltpu.SemaphoreType.DMA((BATCHES + 1, 4)),
+            pltpu.SemaphoreType.DMA((6,)),
+            pltpu.SemaphoreType.DMA((BATCHES + 1, 6)),
         ],
         compiler_params=pltpu.CompilerParams(
             collective_id=0, has_side_effects=True, vmem_limit_bytes=40 * 1024 * 1024

time: 32.9 us -> 30.9 us (0.939)
  Pallas kernels: 32 us -> 30 us
    pallas_call x1, Pallas kernels: 32 us -> 30 us  [on_device(): pl.pallas_call(functools.partial(kernel, shape), out_shape=pltpu.VMEM((ow...]
where the time goes in v2:
time: 30.9 us; the launch traced here: 30.8 us
  Pallas kernels  30 us (97%)
  local copies, waits for them, and re-layouts  0.8 us (3%)
    pallas_call x1, Pallas kernels, on_device(): pl.pallas_call(functools.partial(kernel, shape), out_shape=pltpu.VMEM((ow...  30 us
    unnamed x1, local copies, waits for them, and re-layouts  0.8 us

profile of v2, /device:TPU:0, one launch (start us, length us, event | category | flops | bytes accessed | tf_op | source)
XLA Modules:
  0.0 30.8 jit_solution(4065368072179551765)
XLA Ops:
  0.0 30.0 %shard_map.64 = bf16[128,2048]{1,0:T(8,128)(2,1)S(1)} custom-call(bf16[128,2048]{1,0:T(8,128)(2,1)} %state_hbm.1, s32[1,256]{1,0:T(1,128)} %bitcast.5, s32[1,256]{1,0:T(1,128)} %bitcast.6, s32[1,256]{1,0:T(1,128)} %bitcast.7, s32[1,256]{1,0:T(1,128)} %bitcast.8, f32[1,256]{1,0:T(1,128)} %bitcast.9), custom_call_target="tpu_custom_call" | custom-call | tf_op jit(solution)/shard_map/pallas_call | solution.py:505
  30.0 0.8 %copy.8 = bf16[128,2048]{1,0:T(8,128)(2,1)} copy(bf16[128,2048]{1,0:T(8,128)(2,1)S(1)} %shard_map.64) | data formatting | bytes 1048576

commit v3 on v2

--- a/solution.py
+++ b/solution.py
@@ -12,6 +12,8 @@
 P_SIZE = 128
 BATCHES = 2
 BLOCK = 32
+PANEL = 16
+TILES = 4
 
 FLOOR = math.exp(-2.0)
 F32 = jnp.float32
@@ -60,43 +62,61 @@
         [work[at(v), g * P_SIZE : (g + 1) * P_SIZE] for v in range(size)] for g in range(width)
     ]
     roots = [root[at(v), :] for v in range(size)]
-    cols = [
-        {
-            v: jnp.broadcast_to(parts[0][v][:, r0 + j : r0 + j + 1], (8, P_SIZE))
-            for v in range(j // 8, size)
-        }
-        for j in range(b)
-    ]
-    inside = (lane >= 0) & (lane < b)
-    for v in range(size):
-        unit = jnp.where(lane == row + 8 * v, 1.0, 0.0)
-        parts[0][v] = jnp.where(inside, unit, parts[0][v])
     pivots = [jnp.ones((8, P_SIZE), F32)] * size
-    for j in range(b):
+    for j in range(0, b, 2):
         top, jj = j // 8, j % 8
-        column = cols[j]
-        pivot = spread(column[top], jj)
-        scale = lax.rsqrt(pivot)
-        plain = scale * scale
-        mixed = scale / (pivot * scale + spread(roots[top], jj))
-        pivots[top] = jnp.where(row == jj, column[top], pivots[top])
-        below = dict(column)
-        below[top] = jnp.where(row > jj, column[top], 0.0)
-        first = {v: x * plain for v, x in below.items()}
-        other = {v: x * mixed for v, x in below.items()}
-        for i in range(j + 1, b):
-            s = spread(column[i // 8], i % 8)
+        if j % PANEL == 0:
+            cols = {
+                i: {
+                    v: jnp.broadcast_to(parts[0][v][:, r0 + i : r0 + i + 1], (8, P_SIZE))
+                    for v in range(i // 8, size)
+                }
+                for i in range(j, j + PANEL)
+            }
+            inside = (lane >= j) & (lane < j + PANEL)
+            for v in range(top, size):
+                unit = jnp.where(lane == row + 8 * v, 1.0, 0.0) if 8 * v < j + PANEL else 0.0
+                parts[0][v] = jnp.where(inside, unit, parts[0][v])
+        c0, c1 = cols[j], cols[j + 1]
+        p, q, r = spread(c0[top], jj), spread(c0[top], jj + 1), spread(c1[top], jj + 1)
+        det = p * r - q * q
+        inverse = 1.0 / det
+        root_p, root_d = lax.rsqrt(p), lax.rsqrt(det)
+        cross = q * root_p
+        mix0 = 1.0 / (p * root_p + spread(roots[top], jj))
+        mix1 = 1.0 / (det * root_d * root_p + spread(roots[top], jj + 1))
+        below = cross * mix0
+        after = root_d * root_p * mix1
+        ahead = root_p * mix0
+        left, right, left_m, right_m = {}, {}, {}, {}
+        for v in range(top, size):
+            x, y = r * c0[v] - q * c1[v], p * c1[v] - q * c0[v]
+            left[v], right[v] = x * inverse, y * inverse
+            right_m[v] = y * after
+            left_m[v] = c0[v] * ahead - right_m[v] * below
+        last = row == jj + 1
+        done = row <= jj + 1
+        for x, y, z in ((left, right, cross * root_p), (left_m, right_m, below)):
+            x[top] = jnp.where(done, jnp.where(last, z, 0.0), x[top])
+            y[top] = jnp.where(done, 0.0, y[top])
+        pivots[top] = jnp.where(row == jj, p, pivots[top])
+        pivots[top] = jnp.where(last, det * root_p * root_p, pivots[top])
+        for i in range(j + 2, j - j % PANEL + PANEL):
+            s0, s1 = spread(c0[i // 8], i % 8), spread(c1[i // 8], i % 8)
             for v in range(i // 8, size):
-                cols[i][v] = cols[i][v] - first[v] * s
+                cols[i][v] = cols[i][v] - left[v] * s0 - right[v] * s1
         for g in range(width):
-            line = spread(parts[g][top], jj)
+            s0, s1 = spread(parts[g][top], jj), spread(parts[g][top], jj + 1)
+            x, y = (left_m, right_m) if g else (left, right)
             for v in range(top, size):
-                parts[g][v] = parts[g][v] - (other if g else first)[v] * line
+                parts[g][v] = parts[g][v] - x[v] * s0 - y[v] * s1
     for v in range(size):
         scale = lax.rsqrt(pivots[v])
         mixed = 1.0 / (pivots[v] * scale + roots[v])
         for g in range(width):
             parts[g][v] = parts[g][v] * (mixed if g else scale)
+        ahead = (lane >= (8 * v // PANEL + 1) * PANEL) & (lane < b)
+        parts[0][v] = jnp.where(ahead, 0.0, parts[0][v])
         inv[at(v), :] = jnp.where(lane < b, parts[0][v], 0.0)
         for g in range(1, width):
             solved[at(v), (g - 1) * P_SIZE : g * P_SIZE] = parts[g][v]
@@ -120,7 +140,7 @@
     state_hbm, cen_hbm, half_hbm, rad_hbm, order_hbm, var_hbm,
     out,
     ints, var,
-    e_all, foot, tap, col_c, col_r, var_b, root_b, work, inv, solved, wts, p1, p1_b,
+    e_all, foot, tap, tapers, col_c, col_r, var_b, root_b, work, inv, solved, wts, p1, p1_b,
     part, rs, ag, ag_b, cpart, crs, cag, sizes, sizes_b,
     in_s, e_s, x_s,
 ):
@@ -128,7 +148,6 @@
     n = n_slab * n_sub
     total = n * n_mem
     own, rows = state_hbm.shape
-    part_rows = rows // n_mem
 
     mi = lax.axis_index("mem")
     me = lax.axis_index("slab") * n_sub + lax.axis_index("sub")
@@ -198,35 +217,22 @@
     steep = -2.0 / (width * width)
     height = 1.0 / jnp.sqrt(width)
 
-    def rows_of(mem):
-        return pl.ds(pl.multiple_of(mem * part_rows, part_rows), part_rows)
-
-    my_rows = rows_of(mi)
-
-    half_rows = part_rows // 2
-
-    def half_of(mem, c):
-        return pl.ds(pl.multiple_of(mem * part_rows + c * half_rows, half_rows), half_rows)
-
-    def e_copy(off):
-        to = lax.rem(mi + off, n_mem)
-        at = rows_of(to)
+    size = rows // TILES
+
+    def tile(c):
+        return pl.ds(c * size, size)
+
+    def e_copy(off, c):
         return remote(
-            state_hbm.at[:, at], e_all.at[mi, :, at], e_s.at[0], e_s.at[1], peer(me, to)
+            state_hbm.at[:, tile(c)], e_all.at[mi, :, tile(c)], e_s.at[0], e_s.at[1 + c],
+            peer(me, lax.rem(mi + off, n_mem)),
         )
 
-    def rest_copy(off, c):
-        to = lax.rem(mi + lax.rem(off, n_mem - 1) + 1, n_mem)
-        at = half_of(lax.rem(to + lax.div(off, n_mem - 1) + 1, n_mem), c)
-        return remote(
-            state_hbm.at[:, at], e_all.at[mi, :, at], e_s.at[2 + 2 * c], e_s.at[3 + 2 * c],
-            peer(me, to),
-        )
-
-    def send_rest(c):
-        each(0, (n_mem - 1) * (n_mem - 1), lambda off: rest_copy(off, c).start())
-
-    rest = e_all.at[pl.ds(0, n_mem - 1), :, pl.ds(0, (n_mem - 1) * half_rows)]
+    def send_state(c):
+        each(1, n_mem, lambda off: e_copy(off, c).start())
+
+    def wait_state(c):
+        wait_recv(e_all.at[pl.ds(0, n_mem - 1), :, tile(c)], e_s.at[1 + c])
 
     def project(b):
         lo = b * P_SIZE
@@ -282,10 +288,9 @@
             )
 
         def high_copy(self, off):
-            block = self.high.at[mi * self.owners + self.mine]
-            return remote(
-                block, block, self.sem.at[4], self.sem.at[5], peer(*peer_of(off))
-            )
+            block = self.high.at[self.mine]
+            to = self.device(lax.rem(self.index + off, self.size))
+            return remote(block, block, self.sem.at[4], self.sem.at[5], to)
 
         def finish(self):
             def body():
@@ -304,23 +309,21 @@
 
                     each(1, self.size, add)
                 if self.high is not None:
-                    value = block[...]
-                    high = value.astype(BF16)
-                    self.high[mi * self.owners + self.mine] = high
-                    each(1, total, lambda off: self.high_copy(off).start())
-                    block[...] = value - high.astype(F32)
+                    self.high[self.mine] = block[...].astype(BF16)
+                    each(1, self.size, lambda off: self.high_copy(off).start())
                 each(1, total, lambda off: self.gather_copy(off).start())
 
             self.if_owner(body)
 
-        def gather(self, flat=None, sem=3):
-            flat = self.flat if flat is None else flat
-            count = (n_mem if self.everyone else 1) * self.owners
+        def arrived(self, flat, count, sem):
             self.if_owner(lambda: wait_recv(flat.at[pl.ds(0, count - 1)], self.sem.at[sem]))
             self.if_owner(lambda: wait_recv(flat.at[pl.ds(0, count)], self.sem.at[sem]), False)
 
+        def gather(self):
+            self.arrived(self.flat, (n_mem if self.everyone else 1) * self.owners, 3)
+
         def gather_high(self):
-            self.gather(self.high, 5)
+            self.arrived(self.high, self.owners, 5)
 
         def sent(self):
             self.if_owner(
@@ -329,7 +332,9 @@
             self.if_owner(lambda: wait_sent(self.source, self.sem.at[0]), False)
             self.if_owner(lambda: wait_sent(self.span.at[pl.ds(0, total - 1)], self.sem.at[2]))
             if self.high is not None:
-                self.if_owner(lambda: wait_sent(sizes_b.at[pl.ds(0, total - 1)], self.sem.at[4]))
+                self.if_owner(
+                    lambda: wait_sent(sizes_b.at[pl.ds(0, self.size - 1)], self.sem.at[4])
+                )
 
     owners = part.shape[1]
     projections = [
@@ -347,11 +352,11 @@
     project(0)
     pl.semaphore_wait(barrier, total - 1)
     projections[0].start()
-    each(1, n_mem, lambda off: e_copy(off).start())
+    send_state(0)
     project(1)
     projections[1].start()
     projections[0].finish()
-    send_rest(0)
+    send_state(1)
 
     def slot(b, s):
         return ag[b, s * owners : (s + 1) * owners].reshape(P_SIZE, own)
@@ -371,51 +376,45 @@
             work[:, lo : lo + own] = x
             lo += own
 
-    def taper(b, first, count):
+    def taper(b, at):
         lo = b * P_SIZE
-        row = lax.broadcasted_iota(jnp.int32, (P_SIZE, count), 1) + first
-        c = jnp.concatenate([col_c[lo : lo + P_SIZE, :]] * (count // P_SIZE), axis=1)
-        r = jnp.concatenate([col_r[lo : lo + P_SIZE, :]] * (count // P_SIZE), axis=1)
+        row = lax.broadcasted_iota(jnp.int32, (P_SIZE, size), 1) + at.start
+        c = jnp.concatenate([col_c[lo : lo + P_SIZE, :]] * (size // P_SIZE), axis=1)
+        r = jnp.concatenate([col_r[lo : lo + P_SIZE, :]] * (size // P_SIZE), axis=1)
         near = jnp.maximum(1.0 - jnp.abs(row.astype(F32) - c) * r, 0.0)
         return near * near * (1.0 / (M - 1))
 
+    for b in range(BATCHES):
+        for c in range(TILES):
+            tapers[b, :, tile(c)] = taper(b, tile(c))
+
     projections[0].gather_high()
-    first_b = [ag_b[s * owners : (s + 1) * owners].reshape(P_SIZE, own) for s in range(n_mem)]
-
-    def cross(b, left, at, size):
-        product = 0.0
-        for s in range(n_mem):
-            product = product + jnp.dot(left[s], e_all[s, :, at], preferred_element_type=F32)
-        value = (taper(b, at.start, size) * product).astype(BF16)
-        tap[:, at] = value
-        return value
-
-    def update(at):
-        for s in range(n_mem):
-            moved = jnp.dot(
-                wts[s * own : (s + 1) * own, :], tap[:, at], preferred_element_type=F32
+
+    mine_b = ag_b[...].reshape(P_SIZE, own)
+    change = 0.0
+    for c in range(TILES):
+        product = jnp.dot(mine_b, e_all[mi, :, tile(c)], preferred_element_type=F32)
+        product = tapers[0, :, tile(c)] * product
+        high = product.astype(BF16)
+        low = (product - high.astype(F32)).astype(BF16)
+        for x in (high, low):
+            change = change + lax.dot_general(
+                foot[P_SIZE : 2 * P_SIZE, tile(c)], x, LAST, preferred_element_type=F32
             )
-            e_all[s, :, at] = (e_all[s, :, at].astype(F32) - moved).astype(BF16)
-
-    wait_recv(e_all.at[pl.ds(0, n_mem - 1), :, pl.ds(0, part_rows)], e_s.at[1])
-
-    change = lax.dot_general(
-        foot[P_SIZE : 2 * P_SIZE, my_rows], cross(0, first_b, my_rows, part_rows),
-        LAST, preferred_element_type=F32,
-    )
     cpart[...] = change.reshape(cpart.shape)
     changes.start()
     projections[1].finish()
+    send_state(2)
 
     projections[0].gather()
-    first = [first_b[s].astype(F32) + slot(0, s) for s in range(n_mem)]
+    first = [slot(0, s) for s in range(n_mem)]
     load_work(first, first, 0)
     root_0 = root_b.at[pl.ds(0, P_SIZE)]
     blocks = P_SIZE // BLOCK
     for k in range(blocks // 2):
         block(work, inv, solved, root_0, k)
     changes.finish()
-    send_rest(1)
+    send_state(3)
     for k in range(blocks // 2, blocks):
         block(work, inv, solved, root_0, k)
 
@@ -425,15 +424,25 @@
         ).astype(BF16)
 
     wts[...] = weights(M)
-
-    def others(c):
-        return [half_of(lax.rem(mi + q, n_mem), c) for q in range(1, n_mem)]
-
-    update(my_rows)
-    wait_recv(rest, e_s.at[3])
-    for at in others(0):
-        cross(0, first_b, at, half_rows)
-        update(at)
+    first_b = [slot(0, s).astype(BF16) for s in range(n_mem)]
+
+    def cross(b, left, at):
+        product = 0.0
+        for s in range(n_mem):
+            product = product + jnp.dot(left[s], e_all[s, :, at], preferred_element_type=F32)
+        tap[:, at] = (tapers[b, :, at] * product).astype(BF16)
+
+    def update(at):
+        cross(0, first_b, at)
+        for s in range(n_mem):
+            moved = jnp.dot(
+                wts[s * own : (s + 1) * own, :], tap[:, at], preferred_element_type=F32
+            )
+            e_all[s, :, at] = (e_all[s, :, at].astype(F32) - moved).astype(BF16)
+
+    for c in range(TILES - 1):
+        wait_state(c)
+        update(tile(c))
 
     projections[1].gather()
     changes.gather()
@@ -450,27 +459,15 @@
     alone = own % P_SIZE == 0
     load_work(second, [p1[mi]] if alone else second, 1)
 
-    def beside(k):
-        if k < 2:
-            tiles = [half_of(mi, k)]
-        elif k < 4:
-            tiles = others(k - 2)
-        else:
-            tiles = []
-        for at in tiles:
-            if k == 3:
-                cross(0, first_b, at, half_rows)
-                update(at)
-            cross(1, p1_b, at, half_rows)
-
     used = P_SIZE + (own if alone else M)
     for k in range(blocks):
-        if k == 3:
-            wait_recv(rest, e_s.at[5])
+        if k == TILES - 1:
+            wait_state(k)
+            update(tile(k))
         block(
             work.at[:, pl.ds(0, used)], inv, solved, root_b.at[pl.ds(P_SIZE, P_SIZE)], k
         )
-        beside(k)
+        cross(1, p1_b, tile(k))
     if alone:
         own_w = weights(own)
     else:
@@ -480,9 +477,7 @@
     moved = jnp.dot(own_w, tap[...], preferred_element_type=F32)
     out[...] = (e_all[mi].astype(F32) - moved).astype(BF16)
 
-    wait_sent(e_all.at[pl.ds(0, n_mem - 1), :, pl.ds(0, part_rows)], e_s.at[0])
-    wait_sent(rest, e_s.at[2])
-    wait_sent(rest, e_s.at[4])
+    wait_sent(e_all.at[pl.ds(0, n_mem - 1)], e_s.at[0])
     for x in projections + [changes]:
         x.sent()
 
@@ -513,6 +508,7 @@
             pltpu.VMEM((n_mem, own, rows), BF16),
             pltpu.VMEM((n_obs, rows), BF16),
             pltpu.VMEM((P_SIZE, rows), BF16),
+            pltpu.VMEM((BATCHES, P_SIZE, rows), F32),
             pltpu.VMEM((n_obs, P_SIZE), F32),
             pltpu.VMEM((n_obs, P_SIZE), F32),
             pltpu.VMEM((n_obs, P_SIZE), F32),
@@ -526,14 +522,14 @@
             pltpu.VMEM((BATCHES, owners, chunk, own), F32),
             pltpu.VMEM((BATCHES, n, chunk, own), F32),
             pltpu.VMEM((BATCHES, n_mem * owners, chunk, own), F32),
-            pltpu.VMEM((n_mem * owners, chunk, own), BF16),
+            pltpu.VMEM((owners, chunk, own), BF16),
             pltpu.VMEM((c_owners, c_chunk, P_SIZE), F32),
             pltpu.VMEM((total, c_chunk, P_SIZE), F32),
             pltpu.VMEM((c_owners, c_chunk, P_SIZE), F32),
             pltpu.VMEM((total, chunk, own), F32),
-            pltpu.VMEM((total, chunk, own), BF16),
+            pltpu.VMEM((n, chunk, own), BF16),
             pltpu.SemaphoreType.DMA((3,)),
-            pltpu.SemaphoreType.DMA((6,)),
+            pltpu.SemaphoreType.DMA((1 + TILES,)),
             pltpu.SemaphoreType.DMA((BATCHES + 1, 6)),
         ],
         compiler_params=pltpu.CompilerParams(

time: 30.9 us -> 29.3 us (0.948)
  Pallas kernels: 30 us -> 28.3 us
    pallas_call x1, Pallas kernels: 30 us -> 28.3 us  [on_device(): pl.pallas_call(functools.partial(kernel, shape), out_shape=pltpu.VMEM((ow...]
where the time goes in v3:
time: 29.3 us; the launch traced here: 29.1 us
  Pallas kernels  28.3 us (97%)
  local copies, waits for them, and re-layouts  0.8 us (3%)
    pallas_call x1, Pallas kernels, on_device(): pl.pallas_call(functools.partial(kernel, shape), out_shape=pltpu.VMEM((ow...  28.3 us
    unnamed x1, local copies, waits for them, and re-layouts  0.8 us

profile of v3, /device:TPU:0, one launch (start us, length us, event | category | flops | bytes accessed | tf_op | source)
XLA Modules:
  0.0 29.1 jit_solution(17444372075116460645)
XLA Ops:
  0.0 28.3 %shard_map.64 = bf16[128,2048]{1,0:T(8,128)(2,1)S(1)} custom-call(bf16[128,2048]{1,0:T(8,128)(2,1)} %state_hbm.1, s32[1,256]{1,0:T(1,128)} %bitcast.5, s32[1,256]{1,0:T(1,128)} %bitcast.6, s32[1,256]{1,0:T(1,128)} %bitcast.7, s32[1,256]{1,0:T(1,128)} %bitcast.8, f32[1,256]{1,0:T(1,128)} %bitcast.9), custom_call_target="tpu_custom_call" | custom-call | tf_op jit(solution)/shard_map/pallas_call | solution.py:500
  28.3 0.8 %copy.8 = bf16[128,2048]{1,0:T(8,128)(2,1)} copy(bf16[128,2048]{1,0:T(8,128)(2,1)S(1)} %shard_map.64) | data formatting | bytes 1048576

commit v4 on v3

--- a/solution.py
+++ b/solution.py
@@ -150,7 +150,8 @@
     own, rows = state_hbm.shape
 
     mi = lax.axis_index("mem")
-    me = lax.axis_index("slab") * n_sub + lax.axis_index("sub")
+    slab, sub = lax.axis_index("slab"), lax.axis_index("sub")
+    me = slab * n_sub + sub
 
     def peer(red, mem):
         return {"slab": lax.div(red, n_sub), "sub": lax.rem(red, n_sub), "mem": mem}
@@ -255,13 +256,21 @@
         part[b] = sums.reshape(part.shape[1:])
 
     class Sum:
-        def __init__(self, size, index, device, source, target, result, everyone, sem, flat, span, high=None):
+        def __init__(self, size, index, device, source, target, result, blocks, sem, base, span, high=None):
             self.size, self.index, self.device = size, index, device
-            self.source, self.target, self.result, self.everyone = source, target, result, everyone
-            self.sem, self.flat, self.span, self.high = sem, flat, span, high
+            everyone = blocks is not None
+            self.source, self.target, self.result, self.blocks = source, target, result, blocks
+            self.everyone = everyone
+            self.sems, self.base, self.span, self.high = sem, base, span, high
             self.owners = source.shape[0]
             self.stride = size // self.owners
             self.mine = lax.div(index, self.stride)
+            self.relayed = everyone and self.stride == 1
+            self.sends = (n_slab * n_mem if self.relayed else total) - 1
+            self.handed = (n_sub - 1) * n_slab * n_mem
+
+        def sem(self, k):
+            return self.sems.at[self.base + k]
 
         def if_owner(self, body, owner=True):
             if self.stride == 1:
@@ -274,7 +283,7 @@
             o = lax.rem(self.mine + off, self.owners)
             return remote(
                 self.source.at[o], self.target.at[self.index],
-                self.sem.at[0], self.sem.at[1], self.device(o * self.stride),
+                self.sem(0), self.sem(1), self.device(o * self.stride),
             )
 
         def start(self):
@@ -283,18 +292,32 @@
 
         def gather_copy(self, off):
             block = self.result(mi, self.mine)
-            return remote(
-                block, block, self.sem.at[2], self.sem.at[3], peer(*peer_of(off))
-            )
+            to = peer(*peer_of(off))
+            if self.relayed:
+                to = {
+                    "slab": lax.rem(slab + lax.rem(off, n_slab), n_slab),
+                    "mem": lax.rem(mi + lax.div(off, n_slab), n_mem),
+                }
+            return remote(block, block, self.sem(2), self.sem(3), to)
+
+        def relay_copy(self, off):
+            blocks = self.blocks.at[:, sub]
+            to = {"sub": lax.rem(sub + off, n_sub)}
+            return remote(blocks, blocks, self.sem(4), self.sem(5), to)
+
+        def relay(self):
+            if self.relayed:
+                wait_recv(self.span.at[pl.ds(0, self.sends)], self.sem(3))
+                each(1, n_sub, lambda off: self.relay_copy(off).start())
 
         def high_copy(self, off):
             block = self.high.at[self.mine]
             to = self.device(lax.rem(self.index + off, self.size))
-            return remote(block, block, self.sem.at[4], self.sem.at[5], to)
+            return remote(block, block, self.sem(6), self.sem(7), to)
 
         def finish(self):
             def body():
-                wait_recv(self.target.at[pl.ds(0, self.size - 1)], self.sem.at[1])
+                wait_recv(self.target.at[pl.ds(0, self.size - 1)], self.sem(1))
                 block = self.result(mi, self.mine)
                 if self.size <= 16:
                     value = self.source[self.mine]
@@ -311,62 +334,70 @@
                 if self.high is not None:
                     self.high[self.mine] = block[...].astype(BF16)
                     each(1, self.size, lambda off: self.high_copy(off).start())
-                each(1, total, lambda off: self.gather_copy(off).start())
+                each(1, self.sends + 1, lambda off: self.gather_copy(off).start())
 
             self.if_owner(body)
 
         def arrived(self, flat, count, sem):
-            self.if_owner(lambda: wait_recv(flat.at[pl.ds(0, count - 1)], self.sem.at[sem]))
-            self.if_owner(lambda: wait_recv(flat.at[pl.ds(0, count)], self.sem.at[sem]), False)
+            self.if_owner(lambda: wait_recv(flat.at[pl.ds(0, count - 1)], self.sem(sem)))
+            self.if_owner(lambda: wait_recv(flat.at[pl.ds(0, count)], self.sem(sem)), False)
 
         def gather(self):
-            self.arrived(self.flat, (n_mem if self.everyone else 1) * self.owners, 3)
+            if self.relayed:
+                wait_recv(self.span.at[pl.ds(0, self.handed)], self.sem(5))
+            else:
+                self.arrived(self.span, (n_mem if self.everyone else 1) * self.owners, 3)
 
         def gather_high(self):
-            self.arrived(self.high, self.owners, 5)
+            self.arrived(self.high, self.owners, 7)
 
         def sent(self):
             self.if_owner(
-                lambda: wait_sent(self.source.at[pl.ds(0, self.owners - 1)], self.sem.at[0])
+                lambda: wait_sent(self.source.at[pl.ds(0, self.owners - 1)], self.sem(0))
             )
-            self.if_owner(lambda: wait_sent(self.source, self.sem.at[0]), False)
-            self.if_owner(lambda: wait_sent(self.span.at[pl.ds(0, total - 1)], self.sem.at[2]))
+            self.if_owner(lambda: wait_sent(self.source, self.sem(0)), False)
+            self.if_owner(lambda: wait_sent(self.span.at[pl.ds(0, self.sends)], self.sem(2)))
+            if self.relayed:
+                wait_sent(self.span.at[pl.ds(0, self.handed)], self.sem(4))
             if self.high is not None:
                 self.if_owner(
-                    lambda: wait_sent(sizes_b.at[pl.ds(0, self.size - 1)], self.sem.at[4])
+                    lambda: wait_sent(sizes_b.at[pl.ds(0, self.size - 1)], self.sem(6))
                 )
 
     owners = part.shape[1]
     projections = [
         Sum(
             n, me, lambda i: peer(i, mi), part.at[b], rs.at[b],
-            lambda mem, o, b=b: ag.at[b, mem * owners + o], True, x_s.at[b], ag.at[b], sizes,
-            ag_b if b == 0 else None,
+            lambda mem, o, b=b: ag.at[b, lax.div(mem * owners + o, n_sub), lax.rem(mem * owners + o, n_sub)],
+            ag.at[b], x_s, 8 * b, sizes, ag_b if b == 0 else None,
         )
         for b in range(BATCHES)
     ]
     changes = Sum(
         total, mi * n + me, lambda i: peer(lax.rem(i, n), lax.div(i, n)), cpart, crs,
-        lambda mem, o: cag.at[o], False, x_s.at[BATCHES], cag, crs,
+        lambda mem, o: cag.at[o], None, x_s, 14, crs,
     )
     project(0)
     pl.semaphore_wait(barrier, total - 1)
     projections[0].start()
     send_state(0)
+    send_state(1)
     project(1)
     projections[1].start()
     projections[0].finish()
-    send_state(1)
+    send_state(2)
 
     def slot(b, s):
-        return ag[b, s * owners : (s + 1) * owners].reshape(P_SIZE, own)
+        step = owners // n_sub
+        return ag[b, s * step : (s + 1) * step].reshape(P_SIZE, own)
 
     def load_work(columns, extra, b):
-        cov = 0.0
-        for s in range(n_mem):
-            cov = cov + lax.dot_general(
-                columns[s], columns[s], LAST, precision=HIGH, preferred_element_type=F32
-            )
+        h, m, l = (jnp.concatenate(x, axis=1) for x in zip(*(split3(x) for x in columns)))
+        cov = lax.dot_general(
+            jnp.concatenate([h, h, m, h, m, l], axis=1),
+            jnp.concatenate([h, m, h, l, m, h], axis=1),
+            LAST, preferred_element_type=F32,
+        )
         r = lax.broadcasted_iota(jnp.int32, (P_SIZE, P_SIZE), 0)
         eye = r == lax.broadcasted_iota(jnp.int32, (P_SIZE, P_SIZE), 1)
         v = var_b[b * P_SIZE : (b + 1) * P_SIZE, :]
@@ -404,8 +435,8 @@
     cpart[...] = change.reshape(cpart.shape)
     changes.start()
     projections[1].finish()
-    send_state(2)
-
+
+    projections[0].relay()
     projections[0].gather()
     first = [slot(0, s) for s in range(n_mem)]
     load_work(first, first, 0)
@@ -413,17 +444,21 @@
     blocks = P_SIZE // BLOCK
     for k in range(blocks // 2):
         block(work, inv, solved, root_0, k)
+        if k == 0:
+            send_state(3)
     changes.finish()
-    send_state(3)
     for k in range(blocks // 2, blocks):
         block(work, inv, solved, root_0, k)
 
     def weights(count):
-        return lax.dot_general(
-            solved[:, :count], inv[...], FIRST, precision=HIGH, preferred_element_type=F32
-        ).astype(BF16)
+        h, m, l = split3(solved[:, :count])
+        left = jnp.concatenate([h, h, m, h, m, l], axis=0)
+        h, m, l = split3(inv[...])
+        right = jnp.concatenate([h, m, h, l, m, h], axis=0)
+        return lax.dot_general(left, right, FIRST, preferred_element_type=F32).astype(BF16)
 
     wts[...] = weights(M)
+    projections[1].relay()
     first_b = [slot(0, s).astype(BF16) for s in range(n_mem)]
 
     def cross(b, left, at):
@@ -440,7 +475,7 @@
             )
             e_all[s, :, at] = (e_all[s, :, at].astype(F32) - moved).astype(BF16)
 
-    for c in range(TILES - 1):
+    for c in range(TILES):
         wait_state(c)
         update(tile(c))
 
@@ -461,9 +496,6 @@
 
     used = P_SIZE + (own if alone else M)
     for k in range(blocks):
-        if k == TILES - 1:
-            wait_state(k)
-            update(tile(k))
         block(
             work.at[:, pl.ds(0, used)], inv, solved, root_b.at[pl.ds(P_SIZE, P_SIZE)], k
         )
@@ -521,7 +553,7 @@
             pltpu.VMEM((n_mem, P_SIZE, own), BF16),
             pltpu.VMEM((BATCHES, owners, chunk, own), F32),
             pltpu.VMEM((BATCHES, n, chunk, own), F32),
-            pltpu.VMEM((BATCHES, n_mem * owners, chunk, own), F32),
+            pltpu.VMEM((BATCHES, n_mem * owners // n_sub, n_sub, chunk, own), F32),
             pltpu.VMEM((owners, chunk, own), BF16),
             pltpu.VMEM((c_owners, c_chunk, P_SIZE), F32),
             pltpu.VMEM((total, c_chunk, P_SIZE), F32),
@@ -530,7 +562,7 @@
             pltpu.VMEM((n, chunk, own), BF16),
             pltpu.SemaphoreType.DMA((3,)),
             pltpu.SemaphoreType.DMA((1 + TILES,)),
-            pltpu.SemaphoreType.DMA((BATCHES + 1, 6)),
+            pltpu.SemaphoreType.DMA((18,)),
         ],
         compiler_params=pltpu.CompilerParams(
             collective_id=0, has_side_effects=True, vmem_limit_bytes=40 * 1024 * 1024

time: 29.3 us -> 28.8 us (0.983)
  Pallas kernels: 28.3 us -> 27.9 us
    pallas_call x1, Pallas kernels: 28.3 us -> 27.9 us  [on_device(): pl.pallas_call(functools.partial(kernel, shape), out_shape=pltpu.VMEM((ow...]
where the time goes in v4:
time: 28.8 us; the launch traced here: 28.7 us
  Pallas kernels  27.9 us (97%)
  local copies, waits for them, and re-layouts  0.8 us (3%)
    pallas_call x1, Pallas kernels, on_device(): pl.pallas_call(functools.partial(kernel, shape), out_shape=pltpu.VMEM((ow...  27.9 us
    unnamed x1, local copies, waits for them, and re-layouts  0.8 us

profile of v4, /device:TPU:0, one launch (start us, length us, event | category | flops | bytes accessed | tf_op | source)
XLA Modules:
  0.0 28.7 jit_solution(6520672609347262140)
XLA Ops:
  0.0 27.9 %shard_map.64 = bf16[128,2048]{1,0:T(8,128)(2,1)S(1)} custom-call(bf16[128,2048]{1,0:T(8,128)(2,1)} %state_hbm.1, s32[1,256]{1,0:T(1,128)} %bitcast.5, s32[1,256]{1,0:T(1,128)} %bitcast.6, s32[1,256]{1,0:T(1,128)} %bitcast.7, s32[1,256]{1,0:T(1,128)} %bitcast.8, f32[1,256]{1,0:T(1,128)} %bitcast.9), custom_call_target="tpu_custom_call" | custom-call | tf_op jit(solution)/shard_map/pallas_call | solution.py:532
  27.9 0.8 %copy.8 = bf16[128,2048]{1,0:T(8,128)(2,1)} copy(bf16[128,2048]{1,0:T(8,128)(2,1)S(1)} %shard_map.64) | data formatting | bytes 1048576

commit v5 on v4

--- a/solution.py
+++ b/solution.py
@@ -255,6 +255,9 @@
         )
         part[b] = sums.reshape(part.shape[1:])
 
+    owners = per = part.shape[1]
+    middle = (n - per) // 2
+
     class Sum:
         def __init__(self, size, index, device, source, target, result, blocks, sem, base, span, high=None):
             self.size, self.index, self.device = size, index, device
@@ -263,27 +266,27 @@
             self.everyone = everyone
             self.sems, self.base, self.span, self.high = sem, base, span, high
             self.owners = source.shape[0]
-            self.stride = size // self.owners
-            self.mine = lax.div(index, self.stride)
-            self.relayed = everyone and self.stride == 1
-            self.sends = (n_slab * n_mem if self.relayed else total) - 1
-            self.handed = (n_sub - 1) * n_slab * n_mem
+            self.relayed = everyone
+            self.mine = lax.rem(me + n * per - middle, per) + (0 if everyone else mi * per)
+            self.sends = (n_slab * n_mem if everyone else total) - 1
+            self.direct = n_mem * per // n_sub
+            self.handed = (n_sub - 1) * self.direct
+
+        def owner_of(self, o):
+            return self.device(lax.div(o, per) * n + middle + lax.rem(o, per))
 
         def sem(self, k):
             return self.sems.at[self.base + k]
 
         def if_owner(self, body, owner=True):
-            if self.stride == 1:
-                if owner:
-                    body()
-            else:
-                pl.when((lax.rem(self.index, self.stride) == 0) == owner)(body)
+            inside = jnp.logical_and(me >= middle, me < middle + per)
+            pl.when(inside if owner else jnp.logical_not(inside))(body)
 
         def out_copy(self, off):
             o = lax.rem(self.mine + off, self.owners)
             return remote(
                 self.source.at[o], self.target.at[self.index],
-                self.sem(0), self.sem(1), self.device(o * self.stride),
+                self.sem(0), self.sem(1), self.owner_of(o),
             )
 
         def start(self):
@@ -307,7 +310,7 @@
 
         def relay(self):
             if self.relayed:
-                wait_recv(self.span.at[pl.ds(0, self.sends)], self.sem(3))
+                self.arrived(self.span, self.direct, 3)
                 each(1, n_sub, lambda off: self.relay_copy(off).start())
 
         def high_copy(self, off):
@@ -346,7 +349,7 @@
             if self.relayed:
                 wait_recv(self.span.at[pl.ds(0, self.handed)], self.sem(5))
             else:
-                self.arrived(self.span, (n_mem if self.everyone else 1) * self.owners, 3)
+                self.arrived(self.span, self.owners, 3)
 
         def gather_high(self):
             self.arrived(self.high, self.owners, 7)
@@ -364,7 +367,6 @@
                     lambda: wait_sent(sizes_b.at[pl.ds(0, self.size - 1)], self.sem(6))
                 )
 
-    owners = part.shape[1]
     projections = [
         Sum(
             n, me, lambda i: peer(i, mi), part.at[b], rs.at[b],
@@ -519,9 +521,9 @@
     own, rows = state.shape
     n = n_slab * n_sub
     total = n * n_mem
-    owners = min(n, 8)
+    owners = min(n, 4)
     chunk = P_SIZE // owners
-    c_owners = min(total, 16)
+    c_owners = owners * n_mem
     c_chunk = P_SIZE // c_owners
     n_obs = BATCHES * P_SIZE
     operands = (state,) + tuple(

time: 28.8 us -> 27.7 us (0.962)
  Pallas kernels: 27.9 us -> 26.8 us
    pallas_call x1, Pallas kernels: 27.9 us -> 26.8 us  [on_device(): pl.pallas_call(functools.partial(kernel, shape), out_shape=pltpu.VMEM((ow...]
where the time goes in v5:
time: 27.7 us; the launch traced here: 27.6 us
  Pallas kernels  26.8 us (97%)
  local copies, waits for them, and re-layouts  0.8 us (3%)
    pallas_call x1, Pallas kernels, on_device(): pl.pallas_call(functools.partial(kernel, shape), out_shape=pltpu.VMEM((ow...  26.8 us
    unnamed x1, local copies, waits for them, and re-layouts  0.8 us

profile of v5, /device:TPU:0, one launch (start us, length us, event | category | flops | bytes accessed | tf_op | source)
XLA Modules:
  0.0 27.6 jit_solution(15373965968602877638)
XLA Ops:
  0.0 26.8 %shard_map.64 = bf16[128,2048]{1,0:T(8,128)(2,1)S(1)} custom-call(bf16[128,2048]{1,0:T(8,128)(2,1)} %state_hbm.1, s32[1,256]{1,0:T(1,128)} %bitcast.5, s32[1,256]{1,0:T(1,128)} %bitcast.6, s32[1,256]{1,0:T(1,128)} %bitcast.7, s32[1,256]{1,0:T(1,128)} %bitcast.8, f32[1,256]{1,0:T(1,128)} %bitcast.9), custom_call_target="tpu_custom_call" | custom-call | tf_op jit(solution)/shard_map/pallas_call | solution.py:534
  26.8 0.8 %copy.8 = bf16[128,2048]{1,0:T(8,128)(2,1)} copy(bf16[128,2048]{1,0:T(8,128)(2,1)S(1)} %shard_map.64) | data formatting | bytes 1048576

commit v6 on v5

--- a/solution.py
+++ b/solution.py
@@ -186,13 +186,27 @@
 
     barrier = pltpu.get_barrier_semaphore()
 
-    def greet(off):
-        red, mem = peer_of(off)
-        pl.semaphore_signal(
-            barrier, inc=1, device_id=peer(red, mem), device_id_type=pl.DeviceIdType.MESH
-        )
-
-    each(1, total, greet)
+    owners = per = part.shape[1]
+    middle = (n - per) // 2
+    is_owner = jnp.logical_and(me >= middle, me < middle + per)
+    is_other = jnp.logical_not(is_owner)
+
+    def greet(to):
+        pl.semaphore_signal(barrier, inc=1, device_id=to, device_id_type=pl.DeviceIdType.MESH)
+
+    @pl.when(is_owner)
+    def _():
+        each(1, total, lambda off: greet(peer(*peer_of(off))))
+
+    @pl.when(is_other)
+    def _():
+        each(
+            0, per * n_mem,
+            lambda o: greet(peer(middle + lax.rem(o, per), lax.rem(mi + lax.div(o, per), n_mem))),
+        )
+        each(1, n_mem, lambda off: greet({"mem": lax.rem(mi + off, n_mem)}))
+        each(1, n_sub, lambda off: greet({"sub": lax.rem(sub + off, n_sub)}))
+
     pltpu.make_async_copy(ints, ints, in_s.at[0]).wait()
     var_copy.wait()
 
@@ -254,9 +268,6 @@
             foot[lo : lo + P_SIZE, :], e_all[mi], LAST, preferred_element_type=F32
         )
         part[b] = sums.reshape(part.shape[1:])
-
-    owners = per = part.shape[1]
-    middle = (n - per) // 2
 
     class Sum:
         def __init__(self, size, index, device, source, target, result, blocks, sem, base, span, high=None):
@@ -279,8 +290,7 @@
             return self.sems.at[self.base + k]
 
         def if_owner(self, body, owner=True):
-            inside = jnp.logical_and(me >= middle, me < middle + per)
-            pl.when(inside if owner else jnp.logical_not(inside))(body)
+            pl.when(is_owner if owner else is_other)(body)
 
         def out_copy(self, off):
             o = lax.rem(self.mine + off, self.owners)
@@ -380,14 +390,15 @@
         lambda mem, o: cag.at[o], None, x_s, 14, crs,
     )
     project(0)
-    pl.semaphore_wait(barrier, total - 1)
+    pl.when(is_owner)(lambda: pl.semaphore_wait(barrier, total - 1))
+    pl.when(is_other)(lambda: pl.semaphore_wait(barrier, per * n_mem + n_mem + n_sub - 2))
     projections[0].start()
     send_state(0)
     send_state(1)
     project(1)
     projections[1].start()
     projections[0].finish()
-    send_state(2)
+    pl.when(is_other)(lambda: send_state(2))
 
     def slot(b, s):
         step = owners // n_sub
@@ -421,6 +432,7 @@
         for c in range(TILES):
             tapers[b, :, tile(c)] = taper(b, tile(c))
 
+    projections[1].finish()
     projections[0].gather_high()
 
     mine_b = ag_b[...].reshape(P_SIZE, own)
@@ -436,7 +448,8 @@
             )
     cpart[...] = change.reshape(cpart.shape)
     changes.start()
-    projections[1].finish()
+    pl.when(is_owner)(lambda: send_state(2))
+    pl.when(is_other)(lambda: send_state(3))
 
     projections[0].relay()
     projections[0].gather()
@@ -447,7 +460,7 @@
     for k in range(blocks // 2):
         block(work, inv, solved, root_0, k)
         if k == 0:
-            send_state(3)
+            pl.when(is_owner)(lambda: send_state(3))
     changes.finish()
     for k in range(blocks // 2, blocks):
         block(work, inv, solved, root_0, k)

time: 27.7 us -> 27 us (0.975)
  Pallas kernels: 26.8 us -> 26 us
    pallas_call x1, Pallas kernels: 26.8 us -> 26 us  [on_device(): pl.pallas_call(functools.partial(kernel, shape), out_shape=pltpu.VMEM((ow...]
where the time goes in v6:
time: 27 us; the launch traced here: 26.8 us
  Pallas kernels  26 us (96%)
  local copies, waits for them, and re-layouts  0.8 us (3%)
    pallas_call x1, Pallas kernels, on_device(): pl.pallas_call(functools.partial(kernel, shape), out_shape=pltpu.VMEM((ow...  26 us
    unnamed x1, local copies, waits for them, and re-layouts  0.8 us

profile of v6, /device:TPU:0, one launch (start us, length us, event | category | flops | bytes accessed | tf_op | source)
XLA Modules:
  0.0 26.8 jit_solution(6778559499077370116)
XLA Ops:
  0.0 26.0 %shard_map.64 = bf16[128,2048]{1,0:T(8,128)(2,1)S(1)} custom-call(bf16[128,2048]{1,0:T(8,128)(2,1)} %state_hbm.1, s32[1,256]{1,0:T(1,128)} %bitcast.5, s32[1,256]{1,0:T(1,128)} %bitcast.6, s32[1,256]{1,0:T(1,128)} %bitcast.7, s32[1,256]{1,0:T(1,128)} %bitcast.8, f32[1,256]{1,0:T(1,128)} %bitcast.9), custom_call_target="tpu_custom_call" | custom-call | tf_op jit(solution)/shard_map/pallas_call | solution.py:547
  26.0 0.8 %copy.8 = bf16[128,2048]{1,0:T(8,128)(2,1)} copy(bf16[128,2048]{1,0:T(8,128)(2,1)S(1)} %shard_map.64) | data formatting | bytes 1048576

commit v7 on v6

--- a/solution.py
+++ b/solution.py
@@ -303,6 +303,18 @@
             each(1, self.owners, lambda off: self.out_copy(off).start())
             self.if_owner(lambda: self.out_copy(0).start(), False)
 
+        def start_side(self, q, last):
+            def copy(off):
+                o = q * per + lax.rem(me + n * per - middle + off, per)
+                return remote(
+                    self.source.at[o], self.target.at[self.index],
+                    self.sem(0), self.sem(1), self.owner_of(o),
+                )
+
+            each(1 if last else 0, per, lambda off: copy(off).start())
+            if last:
+                self.if_owner(lambda: copy(0).start(), False)
+
         def gather_copy(self, off):
             block = self.result(mi, self.mine)
             to = peer(*peer_of(off))
@@ -347,7 +359,8 @@
                 if self.high is not None:
                     self.high[self.mine] = block[...].astype(BF16)
                     each(1, self.size, lambda off: self.high_copy(off).start())
-                each(1, self.sends + 1, lambda off: self.gather_copy(off).start())
+                turn = (lambda off: off) if self.relayed else (lambda off: total - off)
+                each(1, self.sends + 1, lambda off: self.gather_copy(turn(off)).start())
 
             self.if_owner(body)
 
@@ -435,19 +448,24 @@
     projections[1].finish()
     projections[0].gather_high()
 
-    mine_b = ag_b[...].reshape(P_SIZE, own)
-    change = 0.0
-    for c in range(TILES):
-        product = jnp.dot(mine_b, e_all[mi, :, tile(c)], preferred_element_type=F32)
-        product = tapers[0, :, tile(c)] * product
-        high = product.astype(BF16)
-        low = (product - high.astype(F32)).astype(BF16)
-        for x in (high, low):
+    side, step = P_SIZE // n_mem, per // n_mem
+    for k in range(1, n_mem + 1):
+        q = lax.rem(mi + k, n_mem)
+        at = pl.ds(pl.multiple_of(q * side, side), side)
+        left = ag_b[pl.ds(q * step, step)].reshape(side, own)
+        change = 0.0
+        for c in range(TILES):
+            product = jnp.dot(left, e_all[mi, :, tile(c)], preferred_element_type=F32)
+            product = tapers[0, at, tile(c)] * product
+            high = product.astype(BF16)
+            low = (product - high.astype(F32)).astype(BF16)
             change = change + lax.dot_general(
-                foot[P_SIZE : 2 * P_SIZE, tile(c)], x, LAST, preferred_element_type=F32
+                jnp.concatenate([high, low], axis=0), foot[P_SIZE : 2 * P_SIZE, tile(c)],
+                LAST, preferred_element_type=F32,
             )
-    cpart[...] = change.reshape(cpart.shape)
-    changes.start()
+        change = change[:side] + change[side:]
+        cpart[pl.ds(q * per, per)] = change.reshape(per, cpart.shape[1], P_SIZE)
+        changes.start_side(q, k == n_mem)
     pl.when(is_owner)(lambda: send_state(2))
     pl.when(is_other)(lambda: send_state(3))
 
@@ -496,7 +514,7 @@
 
     projections[1].gather()
     changes.gather()
-    c_full = jnp.concatenate(split3(cag[...].reshape(P_SIZE, P_SIZE)), axis=0)
+    c_full = jnp.concatenate(split3(cag[...].reshape(P_SIZE, P_SIZE).T), axis=0)
     moved = lax.dot_general(c_full, wts[...], LAST, preferred_element_type=F32)
     moved = moved[:P_SIZE] + (moved[P_SIZE : 2 * P_SIZE] + moved[2 * P_SIZE :])
     second = []

time: 27 us -> 26.7 us (0.989)
  Pallas kernels: 26 us -> 25.7 us
where the time goes in v7:
time: 26.7 us; the launch traced here: 26.6 us
  Pallas kernels  25.7 us (96%)
  local copies, waits for them, and re-layouts  0.8 us (3%)
    pallas_call x1, Pallas kernels, on_device(): pl.pallas_call(functools.partial(kernel, shape), out_shape=pltpu.VMEM((ow...  25.7 us
    unnamed x1, local copies, waits for them, and re-layouts  0.8 us

profile of v7, /device:TPU:0, one launch (start us, length us, event | category | flops | bytes accessed | tf_op | source)
XLA Modules:
  0.0 26.6 jit_solution(4506308529276318773)
XLA Ops:
  0.0 25.7 %shard_map.64 = bf16[128,2048]{1,0:T(8,128)(2,1)S(1)} custom-call(bf16[128,2048]{1,0:T(8,128)(2,1)} %state_hbm.1, s32[1,256]{1,0:T(1,128)} %bitcast.5, s32[1,256]{1,0:T(1,128)} %bitcast.6, s32[1,256]{1,0:T(1,128)} %bitcast.7, s32[1,256]{1,0:T(1,128)} %bitcast.8, f32[1,256]{1,0:T(1,128)} %bitcast.9), custom_call_target="tpu_custom_call" | custom-call | tf_op jit(solution)/shard_map/pallas_call | solution.py:565
  25.8 0.8 %copy.8 = bf16[128,2048]{1,0:T(8,128)(2,1)} copy(bf16[128,2048]{1,0:T(8,128)(2,1)S(1)} %shard_map.64) | data formatting | bytes 1048576

commit v8 on v7

--- a/solution.py
+++ b/solution.py
@@ -409,6 +409,19 @@
     send_state(0)
     send_state(1)
     project(1)
+
+    def taper(b, at):
+        lo = b * P_SIZE
+        row = lax.broadcasted_iota(jnp.int32, (P_SIZE, size), 1) + at.start
+        c = jnp.concatenate([col_c[lo : lo + P_SIZE, :]] * (size // P_SIZE), axis=1)
+        r = jnp.concatenate([col_r[lo : lo + P_SIZE, :]] * (size // P_SIZE), axis=1)
+        near = jnp.maximum(1.0 - jnp.abs(row.astype(F32) - c) * r, 0.0)
+        return near * near * (1.0 / (M - 1))
+
+    for b in range(BATCHES):
+        for c in range(TILES):
+            tapers[b, :, tile(c)] = taper(b, tile(c))
+
     projections[1].start()
     projections[0].finish()
     pl.when(is_other)(lambda: send_state(2))
@@ -432,18 +445,6 @@
         for x in extra:
             work[:, lo : lo + own] = x
             lo += own
-
-    def taper(b, at):
-        lo = b * P_SIZE
-        row = lax.broadcasted_iota(jnp.int32, (P_SIZE, size), 1) + at.start
-        c = jnp.concatenate([col_c[lo : lo + P_SIZE, :]] * (size // P_SIZE), axis=1)
-        r = jnp.concatenate([col_r[lo : lo + P_SIZE, :]] * (size // P_SIZE), axis=1)
-        near = jnp.maximum(1.0 - jnp.abs(row.astype(F32) - c) * r, 0.0)
-        return near * near * (1.0 / (M - 1))
-
-    for b in range(BATCHES):
-        for c in range(TILES):
-            tapers[b, :, tile(c)] = taper(b, tile(c))
 
     projections[1].finish()
     projections[0].gather_high()

time: 26.7 us -> 26.4 us (0.989)
  Pallas kernels: 25.7 us -> 25.4 us
    pallas_call x1, Pallas kernels: 25.7 us -> 25.4 us  [on_device(): pl.pallas_call(functools.partial(kernel, shape), out_shape=pltpu.VMEM((ow...]
where the time goes in v8:
time: 26.4 us; the launch traced here: 26.2 us
  Pallas kernels  25.4 us (96%)
  local copies, waits for them, and re-layouts  0.8 us (3%)
    pallas_call x1, Pallas kernels, on_device(): pl.pallas_call(functools.partial(kernel, shape), out_shape=pltpu.VMEM((ow...  25.4 us
    unnamed x1, local copies, waits for them, and re-layouts  0.8 us

profile of v8, /device:TPU:0, one launch (start us, length us, event | category | flops | bytes accessed | tf_op | source)
XLA Modules:
  0.0 26.2 jit_solution(10570771674969759247)
XLA Ops:
  0.0 25.4 %shard_map.64 = bf16[128,2048]{1,0:T(8,128)(2,1)S(1)} custom-call(bf16[128,2048]{1,0:T(8,128)(2,1)} %state_hbm.1, s32[1,256]{1,0:T(1,128)} %bitcast.5, s32[1,256]{1,0:T(1,128)} %bitcast.6, s32[1,256]{1,0:T(1,128)} %bitcast.7, s32[1,256]{1,0:T(1,128)} %bitcast.8, f32[1,256]{1,0:T(1,128)} %bitcast.9), custom_call_target="tpu_custom_call" | custom-call | tf_op jit(solution)/shard_map/pallas_call | solution.py:566
  25.4 0.8 %copy.8 = bf16[128,2048]{1,0:T(8,128)(2,1)} copy(bf16[128,2048]{1,0:T(8,128)(2,1)S(1)} %shard_map.64) | data formatting | bytes 1048576
